TPU v7x, 256 devices: a whole 4x4x8 slice. The times are simulated.
256 devices in a mesh: frame: 32 (over y_hi, z, core), head: 8 (over x, y_lo).
Axes of the slice: x: 4, y: 4 (y_hi: 2, y_lo: 2; y = y_hi * 2 + y_lo), z: 8, core: 2. Of those that a mesh axis runs over, the one named last changes fastest.
Arguments:
- tokens: bfloat16 [16384, 3072], P(('frame', 'head')), may hold values from -6 to 6
- norm_gain: float32 [3072], replicated, may hold values from 0.25 to 1.75
- w_query: bfloat16 [3072, 2048], P(None, 'head'), may hold values from -0.109375 to 0.109375
- w_key: bfloat16 [3072, 2048], P(None, 'head'), may hold values from -0.109375 to 0.109375
- w_value: bfloat16 [3072, 2048], P(None, 'head'), may hold values from -0.109375 to 0.109375
- query_gain: float32 [128], replicated, may hold values from 0.8 to 2
- key_gain: float32 [128], replicated, may hold values from 0.8 to 2
- w_out: bfloat16 [2048, 3072], P('head'), may hold values from -0.5 to 0.5
- block_lists: int32 [128, 6], P('frame'), may hold values from -1 to 127, as said below
- block_counts: int32 [128], P('frame'), may hold values from 1 to 6, as said below
Outputs:
- attended: bfloat16 [16384, 3072], P(('frame', 'head'))
Inputs may be any that keep to these rules, and one draw needn't show every extreme that they name: `block_lists`: row i holds block_counts[i] distinct key block numbers, then -1 in the remaining slots; its first entry is i itself; every listed j satisfies |j // 4 - i // 4| <= 2. `block_counts`: some row has 6 live entries.
All inputs are finite; a program needn't handle non-finite values.
Results may differ from a plain program's by a relative error of at most 0.019.
Values may be sent and summed in bfloat16 or wider, within the bound.
A program may use at most 64 MiB of HBM per device.

v0:
```python
import jax
import jax.numpy as jnp
from jax import lax
from jax.sharding import PartitionSpec as P

HD = 128
BLK = 128
MAXB = 6


def shifted(shard, axis, by):
    count = lax.axis_size(axis)
    return lax.ppermute(shard, axis, [(i, (i + by) % count) for i in range(count)])


def per_device(
    tokens,
    norm_gain,
    w_query,
    w_key,
    w_value,
    query_gain,
    key_gain,
    w_out,
    block_lists,
    block_counts,
):
    wide = tokens.astype(jnp.float32)
    normed = (
        wide * lax.rsqrt(jnp.mean(wide * wide, axis=-1, keepdims=True) + 1e-06) * norm_gain
    ).astype(jnp.bfloat16)
    local_width = w_query.shape[1]
    local_heads = local_width // HD
    stacked = jnp.concatenate((w_query, w_key, w_value), axis=1)
    projected = jnp.dot(
        lax.all_gather(normed, "head", axis=0, tiled=True),
        stacked,
        preferred_element_type=jnp.float32,
    )
    rows = projected.shape[0]

    def norm_heads(section, gain):
        shaped = section.reshape(rows, local_heads, HD)
        factor = lax.rsqrt(jnp.mean(shaped * shaped, axis=-1, keepdims=True) + 1e-06)
        return (shaped * factor * gain).astype(jnp.bfloat16)

    queries = norm_heads(projected[:, :local_width], query_gain)
    keys = norm_heads(projected[:, local_width : 2 * local_width], key_gain).reshape(
        rows, local_width
    )
    values = projected[:, 2 * local_width :].astype(jnp.bfloat16)
    pairs = jnp.stack((keys, values))
    per_frame = block_lists.shape[0]
    frames = lax.axis_size("frame")
    here = lax.axis_index("frame")
    slot_live = jnp.arange(MAXB, dtype=jnp.int32)[None, :] < block_counts[:, None]
    score_factor = 1.0 / HD**0.5

    def allowed_for(source):
        key_ids = source * per_frame + jnp.arange(per_frame, dtype=jnp.int32)
        hits = (block_lists[:, :, None] == key_ids[None, None, :]) & slot_live[:, :, None]
        coarse = jnp.any(hits, axis=1)
        return jnp.repeat(jnp.repeat(coarse, BLK, axis=0), BLK, axis=1)

    def attend(carry, pair, source):
        weighted, totals = carry
        keys_here = pair[0].reshape(rows, local_heads, HD)
        values_here = pair[1].reshape(rows, local_heads, HD)
        scores = (
            jnp.einsum("qhd,khd->hqk", queries, keys_here, preferred_element_type=jnp.float32)
            * score_factor
        )
        weights = jnp.where(allowed_for(source)[None, :, :], jnp.exp(scores), 0.0)
        totals = totals + jnp.sum(weights, axis=-1)
        weighted = weighted + jnp.einsum(
            "hqk,khd->qhd",
            weights.astype(jnp.bfloat16),
            values_here,
            preferred_element_type=jnp.float32,
        )
        return (weighted, totals)

    start_carry = (
        jnp.zeros((rows, local_heads, HD), jnp.float32),
        jnp.zeros((local_heads, rows), jnp.float32),
    )
    carry = attend(start_carry, pairs, here)

    def one_hop(hop_index, state):
        running, moving = state
        moving = shifted(moving, "frame", 1)
        source = (here - hop_index) % frames
        return (attend(running, moving, source), moving)

    carry, moved = lax.fori_loop(1, frames, one_hop, (carry, pairs))
    weighted, totals = carry
    context = (
        (weighted / jnp.transpose(totals)[:, :, None])
        .astype(jnp.bfloat16)
        .reshape(rows, local_width)
    )
    return lax.psum_scatter(
        jnp.dot(context, w_out, preferred_element_type=jnp.float32).astype(jnp.bfloat16),
        "head",
        scatter_dimension=0,
        tiled=True,
    )


def solution(mesh):
    placed = (
        P(("frame", "head"), None),
        P(),
        P(None, "head"),
        P(None, "head"),
        P(None, "head"),
        P(),
        P(),
        P("head", None),
        P("frame", None),
        P("frame"),
    )
    return jax.shard_map(
        per_device,
        mesh=mesh,
        in_specs=placed,
        out_specs=P(("frame", "head"), None),
        check_vma=False,
    )
```

profile of v0, /device:TPU:16, one launch (start us, length us, event | category | flops | bytes accessed | tf_op | source)
XLA Modules:
  0.0 617.8 jit_solution(17217711991607704642)
XLA Ops:
  12.3 73.4 %all-gather.2.cloned.1.call-done = bf16[512,3072]{1,0:T(8,128)(2,1)} async-done(((bf16[64,3072]{1,0:T(8,128)(2,1)}), bf16[512,3072]{1,0:T(8,128)(2,1)}) %all-gather.2.cloned.1.call-update) | async-done | bytes 3145744 | tf_op jit(solution)/shard_map/all_gather | solution.py:36
  100.5 439.0 %while.20 = (s32[]{:T(128)}, f32[512,2,128]{2,0,1:T(8,128)S(1)}, f32[2,512]{1,0:T(2,128)S(1)}, bf16[2,512,256]{1,2,0:T(8,128)(2,1)S(1)}, s32[4,6]{1,0:T(4,128)S(...) while((s32[]{:T(128)}, f32[512,2,128]{2,0,1:T(8,128)S(1)}, ...), condition=%wide.region_8.9_spmd.clone, body=%wide.region_5.8_spmd.clone.sunk | while | flops 271712576 | bytes 11035182 | solution.py:95
  101.0 11.7 %collective-permute-done = bf16[2,512,256]{1,2,0:T(8,128)(2,1)S(1)} collective-permute-done((bf16[2,512,256]{1,2,0:T(8,128)(2,1)S(1)}, bf16[2,512,256]{1,2,0:T(8,128)(2,1)S(1)}, u32[]{:S(2)}, u32[]{:S(2)}) %collective-permute-start) | collective-permute-done | bytes 524320 | tf_op jit(solution)/shard_map/while/body/eval_jaxpr/ppermute | solution.py:13
  115.2 11.7 %collective-permute-done = bf16[2,512,256]{1,2,0:T(8,128)(2,1)S(1)} collective-permute-done((bf16[2,512,256]{1,2,0:T(8,128)(2,1)S(1)}, bf16[2,512,256]{1,2,0:T(8,128)(2,1)S(1)}, u32[]{:S(2)}, u32[]{:S(2)}) %collective-permute-start) | collective-permute-done | bytes 524320 | tf_op jit(solution)/shard_map/while/body/eval_jaxpr/ppermute | solution.py:13
  129.3 11.7 %collective-permute-done = bf16[2,512,256]{1,2,0:T(8,128)(2,1)S(1)} collective-permute-done((bf16[2,512,256]{1,2,0:T(8,128)(2,1)S(1)}, bf16[2,512,256]{1,2,0:T(8,128)(2,1)S(1)}, u32[]{:S(2)}, u32[]{:S(2)}) %collective-permute-start) | collective-permute-done | bytes 524320 | tf_op jit(solution)/shard_map/while/body/eval_jaxpr/ppermute | solution.py:13
  143.5 11.7 %collective-permute-done = bf16[2,512,256]{1,2,0:T(8,128)(2,1)S(1)} collective-permute-done((bf16[2,512,256]{1,2,0:T(8,128)(2,1)S(1)}, bf16[2,512,256]{1,2,0:T(8,128)(2,1)S(1)}, u32[]{:S(2)}, u32[]{:S(2)}) %collective-permute-start) | collective-permute-done | bytes 524320 | tf_op jit(solution)/shard_map/while/body/eval_jaxpr/ppermute | solution.py:13
  157.7 11.7 %collective-permute-done = bf16[2,512,256]{1,2,0:T(8,128)(2,1)S(1)} collective-permute-done((bf16[2,512,256]{1,2,0:T(8,128)(2,1)S(1)}, bf16[2,512,256]{1,2,0:T(8,128)(2,1)S(1)}, u32[]{:S(2)}, u32[]{:S(2)}) %collective-permute-start) | collective-permute-done | bytes 524320 | tf_op jit(solution)/shard_map/while/body/eval_jaxpr/ppermute | solution.py:13
  171.8 11.7 %collective-permute-done = bf16[2,512,256]{1,2,0:T(8,128)(2,1)S(1)} collective-permute-done((bf16[2,512,256]{1,2,0:T(8,128)(2,1)S(1)}, bf16[2,512,256]{1,2,0:T(8,128)(2,1)S(1)}, u32[]{:S(2)}, u32[]{:S(2)}) %collective-permute-start) | collective-permute-done | bytes 524320 | tf_op jit(solution)/shard_map/while/body/eval_jaxpr/ppermute | solution.py:13
  186.0 11.7 %collective-permute-done = bf16[2,512,256]{1,2,0:T(8,128)(2,1)S(1)} collective-permute-done((bf16[2,512,256]{1,2,0:T(8,128)(2,1)S(1)}, bf16[2,512,256]{1,2,0:T(8,128)(2,1)S(1)}, u32[]{:S(2)}, u32[]{:S(2)}) %collective-permute-start) | collective-permute-done | bytes 524320 | tf_op jit(solution)/shard_map/while/body/eval_jaxpr/ppermute | solution.py:13
  200.1 11.7 %collective-permute-done = bf16[2,512,256]{1,2,0:T(8,128)(2,1)S(1)} collective-permute-done((bf16[2,512,256]{1,2,0:T(8,128)(2,1)S(1)}, bf16[2,512,256]{1,2,0:T(8,128)(2,1)S(1)}, u32[]{:S(2)}, u32[]{:S(2)}) %collective-permute-start) | collective-permute-done | bytes 524320 | tf_op jit(solution)/shard_map/while/body/eval_jaxpr/ppermute | solution.py:13
  214.3 11.7 %collective-permute-done = bf16[2,512,256]{1,2,0:T(8,128)(2,1)S(1)} collective-permute-done((bf16[2,512,256]{1,2,0:T(8,128)(2,1)S(1)}, bf16[2,512,256]{1,2,0:T(8,128)(2,1)S(1)}, u32[]{:S(2)}, u32[]{:S(2)}) %collective-permute-start) | collective-permute-done | bytes 524320 | tf_op jit(solution)/shard_map/while/body/eval_jaxpr/ppermute | solution.py:13
  228.5 11.7 %collective-permute-done = bf16[2,512,256]{1,2,0:T(8,128)(2,1)S(1)} collective-permute-done((bf16[2,512,256]{1,2,0:T(8,128)(2,1)S(1)}, bf16[2,512,256]{1,2,0:T(8,128)(2,1)S(1)}, u32[]{:S(2)}, u32[]{:S(2)}) %collective-permute-start) | collective-permute-done | bytes 524320 | tf_op jit(solution)/shard_map/while/body/eval_jaxpr/ppermute | solution.py:13
  242.6 11.7 %collective-permute-done = bf16[2,512,256]{1,2,0:T(8,128)(2,1)S(1)} collective-permute-done((bf16[2,512,256]{1,2,0:T(8,128)(2,1)S(1)}, bf16[2,512,256]{1,2,0:T(8,128)(2,1)S(1)}, u32[]{:S(2)}, u32[]{:S(2)}) %collective-permute-start) | collective-permute-done | bytes 524320 | tf_op jit(solution)/shard_map/while/body/eval_jaxpr/ppermute | solution.py:13
  256.8 11.7 %collective-permute-done = bf16[2,512,256]{1,2,0:T(8,128)(2,1)S(1)} collective-permute-done((bf16[2,512,256]{1,2,0:T(8,128)(2,1)S(1)}, bf16[2,512,256]{1,2,0:T(8,128)(2,1)S(1)}, u32[]{:S(2)}, u32[]{:S(2)}) %collective-permute-start) | collective-permute-done | bytes 524320 | tf_op jit(solution)/shard_map/while/body/eval_jaxpr/ppermute | solution.py:13
  271.0 11.7 %collective-permute-done = bf16[2,512,256]{1,2,0:T(8,128)(2,1)S(1)} collective-permute-done((bf16[2,512,256]{1,2,0:T(8,128)(2,1)S(1)}, bf16[2,512,256]{1,2,0:T(8,128)(2,1)S(1)}, u32[]{:S(2)}, u32[]{:S(2)}) %collective-permute-start) | collective-permute-done | bytes 524320 | tf_op jit(solution)/shard_map/while/body/eval_jaxpr/ppermute | solution.py:13
  285.1 11.7 %collective-permute-done = bf16[2,512,256]{1,2,0:T(8,128)(2,1)S(1)} collective-permute-done((bf16[2,512,256]{1,2,0:T(8,128)(2,1)S(1)}, bf16[2,512,256]{1,2,0:T(8,128)(2,1)S(1)}, u32[]{:S(2)}, u32[]{:S(2)}) %collective-permute-start) | collective-permute-done | bytes 524320 | tf_op jit(solution)/shard_map/while/body/eval_jaxpr/ppermute | solution.py:13
  299.3 11.7 %collective-permute-done = bf16[2,512,256]{1,2,0:T(8,128)(2,1)S(1)} collective-permute-done((bf16[2,512,256]{1,2,0:T(8,128)(2,1)S(1)}, bf16[2,512,256]{1,2,0:T(8,128)(2,1)S(1)}, u32[]{:S(2)}, u32[]{:S(2)}) %collective-permute-start) | collective-permute-done | bytes 524320 | tf_op jit(solution)/shard_map/while/body/eval_jaxpr/ppermute | solution.py:13
  313.5 11.7 %collective-permute-done = bf16[2,512,256]{1,2,0:T(8,128)(2,1)S(1)} collective-permute-done((bf16[2,512,256]{1,2,0:T(8,128)(2,1)S(1)}, bf16[2,512,256]{1,2,0:T(8,128)(2,1)S(1)}, u32[]{:S(2)}, u32[]{:S(2)}) %collective-permute-start) | collective-permute-done | bytes 524320 | tf_op jit(solution)/shard_map/while/body/eval_jaxpr/ppermute | solution.py:13
  327.6 11.7 %collective-permute-done = bf16[2,512,256]{1,2,0:T(8,128)(2,1)S(1)} collective-permute-done((bf16[2,512,256]{1,2,0:T(8,128)(2,1)S(1)}, bf16[2,512,256]{1,2,0:T(8,128)(2,1)S(1)}, u32[]{:S(2)}, u32[]{:S(2)}) %collective-permute-start) | collective-permute-done | bytes 524320 | tf_op jit(solution)/shard_map/while/body/eval_jaxpr/ppermute | solution.py:13
  341.8 11.7 %collective-permute-done = bf16[2,512,256]{1,2,0:T(8,128)(2,1)S(1)} collective-permute-done((bf16[2,512,256]{1,2,0:T(8,128)(2,1)S(1)}, bf16[2,512,256]{1,2,0:T(8,128)(2,1)S(1)}, u32[]{:S(2)}, u32[]{:S(2)}) %collective-permute-start) | collective-permute-done | bytes 524320 | tf_op jit(solution)/shard_map/while/body/eval_jaxpr/ppermute | solution.py:13
  356.0 11.7 %collective-permute-done = bf16[2,512,256]{1,2,0:T(8,128)(2,1)S(1)} collective-permute-done((bf16[2,512,256]{1,2,0:T(8,128)(2,1)S(1)}, bf16[2,512,256]{1,2,0:T(8,128)(2,1)S(1)}, u32[]{:S(2)}, u32[]{:S(2)}) %collective-permute-start) | collective-permute-done | bytes 524320 | tf_op jit(solution)/shard_map/while/body/eval_jaxpr/ppermute | solution.py:13
  370.1 11.7 %collective-permute-done = bf16[2,512,256]{1,2,0:T(8,128)(2,1)S(1)} collective-permute-done((bf16[2,512,256]{1,2,0:T(8,128)(2,1)S(1)}, bf16[2,512,256]{1,2,0:T(8,128)(2,1)S(1)}, u32[]{:S(2)}, u32[]{:S(2)}) %collective-permute-start) | collective-permute-done | bytes 524320 | tf_op jit(solution)/shard_map/while/body/eval_jaxpr/ppermute | solution.py:13
  384.3 11.7 %collective-permute-done = bf16[2,512,256]{1,2,0:T(8,128)(2,1)S(1)} collective-permute-done((bf16[2,512,256]{1,2,0:T(8,128)(2,1)S(1)}, bf16[2,512,256]{1,2,0:T(8,128)(2,1)S(1)}, u32[]{:S(2)}, u32[]{:S(2)}) %collective-permute-start) | collective-permute-done | bytes 524320 | tf_op jit(solution)/shard_map/while/body/eval_jaxpr/ppermute | solution.py:13
  398.4 11.7 %collective-permute-done = bf16[2,512,256]{1,2,0:T(8,128)(2,1)S(1)} collective-permute-done((bf16[2,512,256]{1,2,0:T(8,128)(2,1)S(1)}, bf16[2,512,256]{1,2,0:T(8,128)(2,1)S(1)}, u32[]{:S(2)}, u32[]{:S(2)}) %collective-permute-start) | collective-permute-done | bytes 524320 | tf_op jit(solution)/shard_map/while/body/eval_jaxpr/ppermute | solution.py:13
  412.6 11.7 %collective-permute-done = bf16[2,512,256]{1,2,0:T(8,128)(2,1)S(1)} collective-permute-done((bf16[2,512,256]{1,2,0:T(8,128)(2,1)S(1)}, bf16[2,512,256]{1,2,0:T(8,128)(2,1)S(1)}, u32[]{:S(2)}, u32[]{:S(2)}) %collective-permute-start) | collective-permute-done | bytes 524320 | tf_op jit(solution)/shard_map/while/body/eval_jaxpr/ppermute | solution.py:13
  426.8 11.7 %collective-permute-done = bf16[2,512,256]{1,2,0:T(8,128)(2,1)S(1)} collective-permute-done((bf16[2,512,256]{1,2,0:T(8,128)(2,1)S(1)}, bf16[2,512,256]{1,2,0:T(8,128)(2,1)S(1)}, u32[]{:S(2)}, u32[]{:S(2)}) %collective-permute-start) | collective-permute-done | bytes 524320 | tf_op jit(solution)/shard_map/while/body/eval_jaxpr/ppermute | solution.py:13
  440.9 11.7 %collective-permute-done = bf16[2,512,256]{1,2,0:T(8,128)(2,1)S(1)} collective-permute-done((bf16[2,512,256]{1,2,0:T(8,128)(2,1)S(1)}, bf16[2,512,256]{1,2,0:T(8,128)(2,1)S(1)}, u32[]{:S(2)}, u32[]{:S(2)}) %collective-permute-start) | collective-permute-done | bytes 524320 | tf_op jit(solution)/shard_map/while/body/eval_jaxpr/ppermute | solution.py:13
  455.1 11.7 %collective-permute-done = bf16[2,512,256]{1,2,0:T(8,128)(2,1)S(1)} collective-permute-done((bf16[2,512,256]{1,2,0:T(8,128)(2,1)S(1)}, bf16[2,512,256]{1,2,0:T(8,128)(2,1)S(1)}, u32[]{:S(2)}, u32[]{:S(2)}) %collective-permute-start) | collective-permute-done | bytes 524320 | tf_op jit(solution)/shard_map/while/body/eval_jaxpr/ppermute | solution.py:13
  469.3 11.7 %collective-permute-done = bf16[2,512,256]{1,2,0:T(8,128)(2,1)S(1)} collective-permute-done((bf16[2,512,256]{1,2,0:T(8,128)(2,1)S(1)}, bf16[2,512,256]{1,2,0:T(8,128)(2,1)S(1)}, u32[]{:S(2)}, u32[]{:S(2)}) %collective-permute-start) | collective-permute-done | bytes 524320 | tf_op jit(solution)/shard_map/while/body/eval_jaxpr/ppermute | solution.py:13
  483.4 11.7 %collective-permute-done = bf16[2,512,256]{1,2,0:T(8,128)(2,1)S(1)} collective-permute-done((bf16[2,512,256]{1,2,0:T(8,128)(2,1)S(1)}, bf16[2,512,256]{1,2,0:T(8,128)(2,1)S(1)}, u32[]{:S(2)}, u32[]{:S(2)}) %collective-permute-start) | collective-permute-done | bytes 524320 | tf_op jit(solution)/shard_map/while/body/eval_jaxpr/ppermute | solution.py:13
  497.6 11.7 %collective-permute-done = bf16[2,512,256]{1,2,0:T(8,128)(2,1)S(1)} collective-permute-done((bf16[2,512,256]{1,2,0:T(8,128)(2,1)S(1)}, bf16[2,512,256]{1,2,0:T(8,128)(2,1)S(1)}, u32[]{:S(2)}, u32[]{:S(2)}) %collective-permute-start) | collective-permute-done | bytes 524320 | tf_op jit(solution)/shard_map/while/body/eval_jaxpr/ppermute | solution.py:13
  542.4 68.5 %reduce-scatter.2.cloned.1.call-done = bf16[64,3072]{1,0:T(8,128)(2,1)} async-done(((bf16[512,3072]{1,0:T(8,128)(2,1)}), bf16[64,3072]{1,0:T(8,128)(2,1)}) %reduce-scatter.2.cloned.1.call-update) | async-done | bytes 393232 | tf_op jit(solution)/shard_map/reduce_scatter | solution.py:102
  (464 shorter events, 120.7 us)
Async XLA Ops:
  6.5 79.2 %all-gather.2.cloned.1.call-start = ((), (), s32[]{:S(2)}) async-start(), calls=%async_computation.1 | async-start | bytes 3538944 | tf_op jit(solution)/shard_map/all_gather | solution.py:36
  9.8 601.2 %reduce-scatter.2.cloned.1.call-start = ((), (), s32[]{:S(2)}) async-start(), calls=%async_computation.2 | async-start | bytes 3538944 | tf_op jit(solution)/shard_map/reduce_scatter | solution.py:102
  114.6 12.3 %collective-permute-start = (bf16[2,512,256]{1,2,0:T(8,128)(2,1)S(1)}, bf16[2,512,256]{1,2,0:T(8,128)(2,1)S(1)}, u32[]{:S(2)}, u32[]{:S(2)}) collective-permute-start(bf16[2,512,256]{1,2,0:T(8,128)(2,1)S(1)} %get-tuple-element.364), channel_id=1, source_target_pairs={{0,8},{8,16},{16,24},{24,32},{32,40},{40,48},{48,56},{56,64},{64,7... | collective-permute-start | bytes 1572872 | tf_op jit(solution)/shard_map/while/body/eval_jaxpr/ppermute | solution.py:13
  128.7 12.3 %collective-permute-start = (bf16[2,512,256]{1,2,0:T(8,128)(2,1)S(1)}, bf16[2,512,256]{1,2,0:T(8,128)(2,1)S(1)}, u32[]{:S(2)}, u32[]{:S(2)}) collective-permute-start(bf16[2,512,256]{1,2,0:T(8,128)(2,1)S(1)} %get-tuple-element.364), channel_id=1, source_target_pairs={{0,8},{8,16},{16,24},{24,32},{32,40},{40,48},{48,56},{56,64},{64,7... | collective-permute-start | bytes 1572872 | tf_op jit(solution)/shard_map/while/body/eval_jaxpr/ppermute | solution.py:13
  142.9 12.3 %collective-permute-start = (bf16[2,512,256]{1,2,0:T(8,128)(2,1)S(1)}, bf16[2,512,256]{1,2,0:T(8,128)(2,1)S(1)}, u32[]{:S(2)}, u32[]{:S(2)}) collective-permute-start(bf16[2,512,256]{1,2,0:T(8,128)(2,1)S(1)} %get-tuple-element.364), channel_id=1, source_target_pairs={{0,8},{8,16},{16,24},{24,32},{32,40},{40,48},{48,56},{56,64},{64,7... | collective-permute-start | bytes 1572872 | tf_op jit(solution)/shard_map/while/body/eval_jaxpr/ppermute | solution.py:13
  157.0 12.3 %collective-permute-start = (bf16[2,512,256]{1,2,0:T(8,128)(2,1)S(1)}, bf16[2,512,256]{1,2,0:T(8,128)(2,1)S(1)}, u32[]{:S(2)}, u32[]{:S(2)}) collective-permute-start(bf16[2,512,256]{1,2,0:T(8,128)(2,1)S(1)} %get-tuple-element.364), channel_id=1, source_target_pairs={{0,8},{8,16},{16,24},{24,32},{32,40},{40,48},{48,56},{56,64},{64,7... | collective-permute-start | bytes 1572872 | tf_op jit(solution)/shard_map/while/body/eval_jaxpr/ppermute | solution.py:13
  171.2 12.3 %collective-permute-start = (bf16[2,512,256]{1,2,0:T(8,128)(2,1)S(1)}, bf16[2,512,256]{1,2,0:T(8,128)(2,1)S(1)}, u32[]{:S(2)}, u32[]{:S(2)}) collective-permute-start(bf16[2,512,256]{1,2,0:T(8,128)(2,1)S(1)} %get-tuple-element.364), channel_id=1, source_target_pairs={{0,8},{8,16},{16,24},{24,32},{32,40},{40,48},{48,56},{56,64},{64,7... | collective-permute-start | bytes 1572872 | tf_op jit(solution)/shard_map/while/body/eval_jaxpr/ppermute | solution.py:13
  185.4 12.3 %collective-permute-start = (bf16[2,512,256]{1,2,0:T(8,128)(2,1)S(1)}, bf16[2,512,256]{1,2,0:T(8,128)(2,1)S(1)}, u32[]{:S(2)}, u32[]{:S(2)}) collective-permute-start(bf16[2,512,256]{1,2,0:T(8,128)(2,1)S(1)} %get-tuple-element.364), channel_id=1, source_target_pairs={{0,8},{8,16},{16,24},{24,32},{32,40},{40,48},{48,56},{56,64},{64,7... | collective-permute-start | bytes 1572872 | tf_op jit(solution)/shard_map/while/body/eval_jaxpr/ppermute | solution.py:13
  199.5 12.3 %collective-permute-start = (bf16[2,512,256]{1,2,0:T(8,128)(2,1)S(1)}, bf16[2,512,256]{1,2,0:T(8,128)(2,1)S(1)}, u32[]{:S(2)}, u32[]{:S(2)}) collective-permute-start(bf16[2,512,256]{1,2,0:T(8,128)(2,1)S(1)} %get-tuple-element.364), channel_id=1, source_target_pairs={{0,8},{8,16},{16,24},{24,32},{32,40},{40,48},{48,56},{56,64},{64,7... | collective-permute-start | bytes 1572872 | tf_op jit(solution)/shard_map/while/body/eval_jaxpr/ppermute | solution.py:13
  213.7 12.3 %collective-permute-start = (bf16[2,512,256]{1,2,0:T(8,128)(2,1)S(1)}, bf16[2,512,256]{1,2,0:T(8,128)(2,1)S(1)}, u32[]{:S(2)}, u32[]{:S(2)}) collective-permute-start(bf16[2,512,256]{1,2,0:T(8,128)(2,1)S(1)} %get-tuple-element.364), channel_id=1, source_target_pairs={{0,8},{8,16},{16,24},{24,32},{32,40},{40,48},{48,56},{56,64},{64,7... | collective-permute-start | bytes 1572872 | tf_op jit(solution)/shard_map/while/body/eval_jaxpr/ppermute | solution.py:13
  227.9 12.3 %collective-permute-start = (bf16[2,512,256]{1,2,0:T(8,128)(2,1)S(1)}, bf16[2,512,256]{1,2,0:T(8,128)(2,1)S(1)}, u32[]{:S(2)}, u32[]{:S(2)}) collective-permute-start(bf16[2,512,256]{1,2,0:T(8,128)(2,1)S(1)} %get-tuple-element.364), channel_id=1, source_target_pairs={{0,8},{8,16},{16,24},{24,32},{32,40},{40,48},{48,56},{56,64},{64,7... | collective-permute-start | bytes 1572872 | tf_op jit(solution)/shard_map/while/body/eval_jaxpr/ppermute | solution.py:13
  242.0 12.3 %collective-permute-start = (bf16[2,512,256]{1,2,0:T(8,128)(2,1)S(1)}, bf16[2,512,256]{1,2,0:T(8,128)(2,1)S(1)}, u32[]{:S(2)}, u32[]{:S(2)}) collective-permute-start(bf16[2,512,256]{1,2,0:T(8,128)(2,1)S(1)} %get-tuple-element.364), channel_id=1, source_target_pairs={{0,8},{8,16},{16,24},{24,32},{32,40},{40,48},{48,56},{56,64},{64,7... | collective-permute-start | bytes 1572872 | tf_op jit(solution)/shard_map/while/body/eval_jaxpr/ppermute | solution.py:13
  256.2 12.3 %collective-permute-start = (bf16[2,512,256]{1,2,0:T(8,128)(2,1)S(1)}, bf16[2,512,256]{1,2,0:T(8,128)(2,1)S(1)}, u32[]{:S(2)}, u32[]{:S(2)}) collective-permute-start(bf16[2,512,256]{1,2,0:T(8,128)(2,1)S(1)} %get-tuple-element.364), channel_id=1, source_target_pairs={{0,8},{8,16},{16,24},{24,32},{32,40},{40,48},{48,56},{56,64},{64,7... | collective-permute-start | bytes 1572872 | tf_op jit(solution)/shard_map/while/body/eval_jaxpr/ppermute | solution.py:13
  270.3 12.3 %collective-permute-start = (bf16[2,512,256]{1,2,0:T(8,128)(2,1)S(1)}, bf16[2,512,256]{1,2,0:T(8,128)(2,1)S(1)}, u32[]{:S(2)}, u32[]{:S(2)}) collective-permute-start(bf16[2,512,256]{1,2,0:T(8,128)(2,1)S(1)} %get-tuple-element.364), channel_id=1, source_target_pairs={{0,8},{8,16},{16,24},{24,32},{32,40},{40,48},{48,56},{56,64},{64,7... | collective-permute-start | bytes 1572872 | tf_op jit(solution)/shard_map/while/body/eval_jaxpr/ppermute | solution.py:13
  284.5 12.3 %collective-permute-start = (bf16[2,512,256]{1,2,0:T(8,128)(2,1)S(1)}, bf16[2,512,256]{1,2,0:T(8,128)(2,1)S(1)}, u32[]{:S(2)}, u32[]{:S(2)}) collective-permute-start(bf16[2,512,256]{1,2,0:T(8,128)(2,1)S(1)} %get-tuple-element.364), channel_id=1, source_target_pairs={{0,8},{8,16},{16,24},{24,32},{32,40},{40,48},{48,56},{56,64},{64,7... | collective-permute-start | bytes 1572872 | tf_op jit(solution)/shard_map/while/body/eval_jaxpr/ppermute | solution.py:13
  298.7 12.3 %collective-permute-start = (bf16[2,512,256]{1,2,0:T(8,128)(2,1)S(1)}, bf16[2,512,256]{1,2,0:T(8,128)(2,1)S(1)}, u32[]{:S(2)}, u32[]{:S(2)}) collective-permute-start(bf16[2,512,256]{1,2,0:T(8,128)(2,1)S(1)} %get-tuple-element.364), channel_id=1, source_target_pairs={{0,8},{8,16},{16,24},{24,32},{32,40},{40,48},{48,56},{56,64},{64,7... | collective-permute-start | bytes 1572872 | tf_op jit(solution)/shard_map/while/body/eval_jaxpr/ppermute | solution.py:13
  312.8 12.3 %collective-permute-start = (bf16[2,512,256]{1,2,0:T(8,128)(2,1)S(1)}, bf16[2,512,256]{1,2,0:T(8,128)(2,1)S(1)}, u32[]{:S(2)}, u32[]{:S(2)}) collective-permute-start(bf16[2,512,256]{1,2,0:T(8,128)(2,1)S(1)} %get-tuple-element.364), channel_id=1, source_target_pairs={{0,8},{8,16},{16,24},{24,32},{32,40},{40,48},{48,56},{56,64},{64,7... | collective-permute-start | bytes 1572872 | tf_op jit(solution)/shard_map/while/body/eval_jaxpr/ppermute | solution.py:13
  327.0 12.3 %collective-permute-start = (bf16[2,512,256]{1,2,0:T(8,128)(2,1)S(1)}, bf16[2,512,256]{1,2,0:T(8,128)(2,1)S(1)}, u32[]{:S(2)}, u32[]{:S(2)}) collective-permute-start(bf16[2,512,256]{1,2,0:T(8,128)(2,1)S(1)} %get-tuple-element.364), channel_id=1, source_target_pairs={{0,8},{8,16},{16,24},{24,32},{32,40},{40,48},{48,56},{56,64},{64,7... | collective-permute-start | bytes 1572872 | tf_op jit(solution)/shard_map/while/body/eval_jaxpr/ppermute | solution.py:13
  341.2 12.3 %collective-permute-start = (bf16[2,512,256]{1,2,0:T(8,128)(2,1)S(1)}, bf16[2,512,256]{1,2,0:T(8,128)(2,1)S(1)}, u32[]{:S(2)}, u32[]{:S(2)}) collective-permute-start(bf16[2,512,256]{1,2,0:T(8,128)(2,1)S(1)} %get-tuple-element.364), channel_id=1, source_target_pairs={{0,8},{8,16},{16,24},{24,32},{32,40},{40,48},{48,56},{56,64},{64,7... | collective-permute-start | bytes 1572872 | tf_op jit(solution)/shard_map/while/body/eval_jaxpr/ppermute | solution.py:13
  355.3 12.3 %collective-permute-start = (bf16[2,512,256]{1,2,0:T(8,128)(2,1)S(1)}, bf16[2,512,256]{1,2,0:T(8,128)(2,1)S(1)}, u32[]{:S(2)}, u32[]{:S(2)}) collective-permute-start(bf16[2,512,256]{1,2,0:T(8,128)(2,1)S(1)} %get-tuple-element.364), channel_id=1, source_target_pairs={{0,8},{8,16},{16,24},{24,32},{32,40},{40,48},{48,56},{56,64},{64,7... | collective-permute-start | bytes 1572872 | tf_op jit(solution)/shard_map/while/body/eval_jaxpr/ppermute | solution.py:13
  369.5 12.3 %collective-permute-start = (bf16[2,512,256]{1,2,0:T(8,128)(2,1)S(1)}, bf16[2,512,256]{1,2,0:T(8,128)(2,1)S(1)}, u32[]{:S(2)}, u32[]{:S(2)}) collective-permute-start(bf16[2,512,256]{1,2,0:T(8,128)(2,1)S(1)} %get-tuple-element.364), channel_id=1, source_target_pairs={{0,8},{8,16},{16,24},{24,32},{32,40},{40,48},{48,56},{56,64},{64,7... | collective-permute-start | bytes 1572872 | tf_op jit(solution)/shard_map/while/body/eval_jaxpr/ppermute | solution.py:13
  383.7 12.3 %collective-permute-start = (bf16[2,512,256]{1,2,0:T(8,128)(2,1)S(1)}, bf16[2,512,256]{1,2,0:T(8,128)(2,1)S(1)}, u32[]{:S(2)}, u32[]{:S(2)}) collective-permute-start(bf16[2,512,256]{1,2,0:T(8,128)(2,1)S(1)} %get-tuple-element.364), channel_id=1, source_target_pairs={{0,8},{8,16},{16,24},{24,32},{32,40},{40,48},{48,56},{56,64},{64,7... | collective-permute-start | bytes 1572872 | tf_op jit(solution)/shard_map/while/body/eval_jaxpr/ppermute | solution.py:13
  397.8 12.3 %collective-permute-start = (bf16[2,512,256]{1,2,0:T(8,128)(2,1)S(1)}, bf16[2,512,256]{1,2,0:T(8,128)(2,1)S(1)}, u32[]{:S(2)}, u32[]{:S(2)}) collective-permute-start(bf16[2,512,256]{1,2,0:T(8,128)(2,1)S(1)} %get-tuple-element.364), channel_id=1, source_target_pairs={{0,8},{8,16},{16,24},{24,32},{32,40},{40,48},{48,56},{56,64},{64,7... | collective-permute-start | bytes 1572872 | tf_op jit(solution)/shard_map/while/body/eval_jaxpr/ppermute | solution.py:13
  412.0 12.3 %collective-permute-start = (bf16[2,512,256]{1,2,0:T(8,128)(2,1)S(1)}, bf16[2,512,256]{1,2,0:T(8,128)(2,1)S(1)}, u32[]{:S(2)}, u32[]{:S(2)}) collective-permute-start(bf16[2,512,256]{1,2,0:T(8,128)(2,1)S(1)} %get-tuple-element.364), channel_id=1, source_target_pairs={{0,8},{8,16},{16,24},{24,32},{32,40},{40,48},{48,56},{56,64},{64,7... | collective-permute-start | bytes 1572872 | tf_op jit(solution)/shard_map/while/body/eval_jaxpr/ppermute | solution.py:13
  426.2 12.3 %collective-permute-start = (bf16[2,512,256]{1,2,0:T(8,128)(2,1)S(1)}, bf16[2,512,256]{1,2,0:T(8,128)(2,1)S(1)}, u32[]{:S(2)}, u32[]{:S(2)}) collective-permute-start(bf16[2,512,256]{1,2,0:T(8,128)(2,1)S(1)} %get-tuple-element.364), channel_id=1, source_target_pairs={{0,8},{8,16},{16,24},{24,32},{32,40},{40,48},{48,56},{56,64},{64,7... | collective-permute-start | bytes 1572872 | tf_op jit(solution)/shard_map/while/body/eval_jaxpr/ppermute | solution.py:13
  440.3 12.3 %collective-permute-start = (bf16[2,512,256]{1,2,0:T(8,128)(2,1)S(1)}, bf16[2,512,256]{1,2,0:T(8,128)(2,1)S(1)}, u32[]{:S(2)}, u32[]{:S(2)}) collective-permute-start(bf16[2,512,256]{1,2,0:T(8,128)(2,1)S(1)} %get-tuple-element.364), channel_id=1, source_target_pairs={{0,8},{8,16},{16,24},{24,32},{32,40},{40,48},{48,56},{56,64},{64,7... | collective-permute-start | bytes 1572872 | tf_op jit(solution)/shard_map/while/body/eval_jaxpr/ppermute | solution.py:13
  454.5 12.3 %collective-permute-start = (bf16[2,512,256]{1,2,0:T(8,128)(2,1)S(1)}, bf16[2,512,256]{1,2,0:T(8,128)(2,1)S(1)}, u32[]{:S(2)}, u32[]{:S(2)}) collective-permute-start(bf16[2,512,256]{1,2,0:T(8,128)(2,1)S(1)} %get-tuple-element.364), channel_id=1, source_target_pairs={{0,8},{8,16},{16,24},{24,32},{32,40},{40,48},{48,56},{56,64},{64,7... | collective-permute-start | bytes 1572872 | tf_op jit(solution)/shard_map/while/body/eval_jaxpr/ppermute | solution.py:13
  468.6 12.3 %collective-permute-start = (bf16[2,512,256]{1,2,0:T(8,128)(2,1)S(1)}, bf16[2,512,256]{1,2,0:T(8,128)(2,1)S(1)}, u32[]{:S(2)}, u32[]{:S(2)}) collective-permute-start(bf16[2,512,256]{1,2,0:T(8,128)(2,1)S(1)} %get-tuple-element.364), channel_id=1, source_target_pairs={{0,8},{8,16},{16,24},{24,32},{32,40},{40,48},{48,56},{56,64},{64,7... | collective-permute-start | bytes 1572872 | tf_op jit(solution)/shard_map/while/body/eval_jaxpr/ppermute | solution.py:13
  482.8 12.3 %collective-permute-start = (bf16[2,512,256]{1,2,0:T(8,128)(2,1)S(1)}, bf16[2,512,256]{1,2,0:T(8,128)(2,1)S(1)}, u32[]{:S(2)}, u32[]{:S(2)}) collective-permute-start(bf16[2,512,256]{1,2,0:T(8,128)(2,1)S(1)} %get-tuple-element.364), channel_id=1, source_target_pairs={{0,8},{8,16},{16,24},{24,32},{32,40},{40,48},{48,56},{56,64},{64,7... | collective-permute-start | bytes 1572872 | tf_op jit(solution)/shard_map/while/body/eval_jaxpr/ppermute | solution.py:13
  497.0 12.3 %collective-permute-start = (bf16[2,512,256]{1,2,0:T(8,128)(2,1)S(1)}, bf16[2,512,256]{1,2,0:T(8,128)(2,1)S(1)}, u32[]{:S(2)}, u32[]{:S(2)}) collective-permute-start(bf16[2,512,256]{1,2,0:T(8,128)(2,1)S(1)} %get-tuple-element.364), channel_id=1, source_target_pairs={{0,8},{8,16},{16,24},{24,32},{32,40},{40,48},{48,56},{56,64},{64,7... | collective-permute-start | bytes 1572872 | tf_op jit(solution)/shard_map/while/body/eval_jaxpr/ppermute | solution.py:13
  511.1 12.3 %collective-permute-start = (bf16[2,512,256]{1,2,0:T(8,128)(2,1)S(1)}, bf16[2,512,256]{1,2,0:T(8,128)(2,1)S(1)}, u32[]{:S(2)}, u32[]{:S(2)}) collective-permute-start(bf16[2,512,256]{1,2,0:T(8,128)(2,1)S(1)} %get-tuple-element.364), channel_id=1, source_target_pairs={{0,8},{8,16},{16,24},{24,32},{32,40},{40,48},{48,56},{56,64},{64,7... | collective-permute-start | bytes 1572872 | tf_op jit(solution)/shard_map/while/body/eval_jaxpr/ppermute | solution.py:13
  525.3 12.3 %collective-permute-start = (bf16[2,512,256]{1,2,0:T(8,128)(2,1)S(1)}, bf16[2,512,256]{1,2,0:T(8,128)(2,1)S(1)}, u32[]{:S(2)}, u32[]{:S(2)}) collective-permute-start(bf16[2,512,256]{1,2,0:T(8,128)(2,1)S(1)} %get-tuple-element.364), channel_id=1, source_target_pairs={{0,8},{8,16},{16,24},{24,32},{32,40},{40,48},{48,56},{56,64},{64,7... | collective-permute-start | bytes 1572872 | tf_op jit(solution)/shard_map/while/body/eval_jaxpr/ppermute | solution.py:13
  (11 other events, 557.7 us)
Sparse Core Ops, SparseCore 0:
  9.9 75.7 all-gather.1
  542.6 68.3 reduce-scatter.1
where the time goes:
time: 619 us; the launch traced here: 618 us
  waiting for transfers between devices  504 us (81%)
  matrix products  61.6 us (10%)
  other arithmetic  17.3 us (3%)
  local copies, waits for them, and re-layouts  16 us (3%)
  between operations  13.7 us (2%)
    ppermute x31, waiting for transfers between devices, shifted(): lax.ppermute(shard, axis, [(i, (i + by) % count) for i in range(count)])  362 us
    all_gather x1, waiting for transfers between devices, per_device(): lax.all_gather(normed, 'head', axis=0, tiled=True)  73.4 us
    reduce_scatter x1, waiting for transfers between devices, per_device(): lax.psum_scatter(jnp.dot(context, w_out, preferred_element_type=jnp.float...  68.5 us
    dot_general x32, matrix products, attend(): jnp.einsum('hqk,khd->qhd', weights.astype(jnp.bfloat16), values_here, pre...  27.5 us
    dot_general x32, matrix products, attend(): jnp.einsum('qhd,khd->hqk', queries, keys_here, preferred_element_type=jnp...  25.5 us
  transfers between devices with their start and end apart: 33, of which 33 were waited for; matrix products, arithmetic and copies ran while one was open for 3% of the time, Pallas kernels for 0%

commit v1 on v0

v1 whole, which is shorter than its diff:
```python
import functools

import jax
import jax.numpy as jnp
from jax import lax
from jax.experimental import pallas as pl
from jax.experimental.pallas import tpu as pltpu
from jax.sharding import PartitionSpec as P

HD = 128
BLK = 128
MAXB = 6
BAND = 2
EPS = 1e-06
MESH = pl.DeviceIdType.MESH


def kernel(
    frames,
    tokens_ref,
    ngain_ref,
    qgain_ref,
    kgain_ref,
    lists_ref,
    counts_ref,
    wq_hbm,
    wk_hbm,
    wv_hbm,
    wo_hbm,
    out_ref,
    wq,
    wk,
    wv,
    wo,
    xn,
    q,
    kv,
    part,
    got_a,
    got_h,
    got_b,
    got_c,
    got_d,
    w_sem,
    ag_s,
    ag_r,
    kv_s,
    kv_r,
    rs_s,
    rs_r,
):
    f = lax.axis_index("frame")
    head = lax.axis_index("head")
    x, y = head // 2, head % 2
    other = 1 - y
    right, left, opposite = (x + 1) % 4, (x + 3) % 4, (x + 2) % 4
    dev_right, dev_left, dev_other = right * 2 + y, left * 2 + y, x * 2 + other
    rows = tokens_ref.shape[0]
    half = rows // 2
    width = wq.shape[1]
    heads = width // HD
    reach = [d for d in range(-BAND, BAND + 1) if d != 0]

    weights = [
        pltpu.make_async_copy(src, dst, w_sem.at[i])
        for i, (src, dst) in enumerate(((wq_hbm, wq), (wk_hbm, wk), (wv_hbm, wv), (wo_hbm, wo)))
    ]
    for copy in weights:
        copy.start()

    def within(d):
        return jnp.logical_and(f + d >= 0, f + d < frames)

    barrier = pltpu.get_barrier_semaphore()
    for device in (dev_right, dev_left, dev_other):
        pl.semaphore_signal(barrier, inc=1, device_id={"head": device}, device_id_type=MESH)
    for d in reach:

        @pl.when(within(d))
        def _():
            pl.semaphore_signal(barrier, inc=1, device_id={"frame": f + d}, device_id_type=MESH)

    wide = tokens_ref[...].astype(jnp.float32)
    factor = lax.rsqrt(jnp.mean(wide * wide, axis=-1, keepdims=True) + EPS)
    xn[0] = (wide * factor * ngain_ref[...]).astype(jnp.bfloat16)

    peers = 3
    for d in reach:
        peers = peers + jnp.where(within(d), 1, 0)
    pl.semaphore_wait(barrier, peers)

    def send(src, dst, sems, index, device):
        return pltpu.make_async_remote_copy(
            src_ref=src,
            dst_ref=dst,
            send_sem=sems[0].at[index],
            recv_sem=sems[1].at[index],
            device_id={"head": device},
            device_id_type=MESH,
        )

    ag = (ag_s, ag_r)
    low, high = pl.ds(0, half), pl.ds(half, half)
    a_right = send(xn.at[0], xn.at[2], ag, 0, dev_right)
    a_left = send(xn.at[0], xn.at[3], ag, 1, dev_left)
    b_other = send(xn.at[0], xn.at[1], ag, 2, dev_other)
    f_right = send(xn.at[2, high], xn.at[4, high], ag, 3, dev_right)
    f_left = send(xn.at[3, low], xn.at[4, low], ag, 4, dev_left)
    c_right = send(xn.at[1], xn.at[5], ag, 5, dev_right)
    c_left = send(xn.at[1], xn.at[6], ag, 6, dev_left)
    d_high = send(xn.at[4, high], xn.at[7, high], ag, 7, dev_other)
    d_low = send(xn.at[4, low], xn.at[7, low], ag, 8, dev_other)

    slot_head = [
        head,
        dev_other,
        dev_left,
        dev_right,
        opposite * 2 + y,
        left * 2 + other,
        right * 2 + other,
        opposite * 2 + other,
    ]

    def normed_heads(section, gain_ref):
        done = []
        for i in range(heads):
            part_i = section[:, i * HD : (i + 1) * HD]
            scale = lax.rsqrt(jnp.mean(part_i * part_i, axis=-1, keepdims=True) + EPS)
            done.append((part_i * scale * gain_ref[...]).astype(jnp.bfloat16))
        return done

    def project(slot):
        at = slot_head[slot]
        mine = BAND * 8 + at
        block = xn[slot]
        keys = jnp.dot(block, wk[...], preferred_element_type=jnp.float32)
        for i, piece in enumerate(normed_heads(keys, kgain_ref)):
            kv[mine, :, i * HD : (i + 1) * HD] = piece
        values = jnp.dot(block, wv[...], preferred_element_type=jnp.float32)
        kv[mine, :, width:] = values.astype(jnp.bfloat16)
        for i, d in enumerate(reach):

            @pl.when(within(d))
            def _():
                pltpu.make_async_remote_copy(
                    src_ref=kv.at[mine],
                    dst_ref=kv.at[(BAND - d) * 8 + at],
                    send_sem=kv_s.at[i],
                    recv_sem=kv_r.at[i],
                    device_id={"frame": f + d},
                    device_id_type=MESH,
                ).start()

        queries = jnp.dot(block, wq[...], preferred_element_type=jnp.float32)
        for i, piece in enumerate(normed_heads(queries, qgain_ref)):
            q[at, :, i * HD : (i + 1) * HD] = piece

    a_right.start()
    a_left.start()
    b_other.start()
    for copy in weights:
        copy.wait()
    project(0)
    b_other.wait_recv()
    c_right.start()
    c_left.start()
    a_right.wait_recv()
    f_right.start()
    a_left.wait_recv()
    f_left.start()
    project(1)
    project(2)
    project(3)
    f_right.wait_recv()
    d_high.start()
    f_left.wait_recv()
    d_low.start()
    project(4)
    c_right.wait_recv()
    project(5)
    c_left.wait_recv()
    project(6)
    d_high.wait_recv()
    d_low.wait_recv()
    project(7)

    def frame_copy(i, d):
        return pltpu.make_async_remote_copy(
            src_ref=kv.at[pl.ds(BAND * 8, 8)],
            dst_ref=kv.at[pl.ds((BAND - d) * 8, 8)],
            send_sem=kv_s.at[i],
            recv_sem=kv_r.at[i],
            device_id={"frame": f + d},
            device_id_type=MESH,
        )

    for i, d in enumerate(reach):

        @pl.when(within(-d))
        def _():
            frame_copy(i, d).wait_recv()

    score_factor = 1.0 / HD**0.5

    def attend(block, place):
        queries = q[pl.ds(block * 2, 2)].reshape(BLK, width)
        listed = counts_ref[block]
        weighted = [jnp.zeros((BLK, HD), jnp.float32) for _ in range(heads)]
        totals = [jnp.zeros((BLK, 1), jnp.float32) for _ in range(heads)]
        for m in range(MAXB):
            live = m < listed
            picked = jnp.where(live, lists_ref[block, m] - f * 4 + BAND * 4, BAND * 4 + block)
            picked = jnp.clip(picked, 0, 5 * 4 - 1)
            pair = kv[pl.ds(picked * 2, 2)].reshape(BLK, 2 * width)
            on = jnp.where(live, 1.0, 0.0).astype(jnp.float32)
            for i in range(heads):
                scores = lax.dot_general(
                    queries[:, i * HD : (i + 1) * HD],
                    pair[:, i * HD : (i + 1) * HD],
                    (((1,), (1,)), ((), ())),
                    preferred_element_type=jnp.float32,
                )
                weight = jnp.exp(scores * score_factor) * on
                totals[i] = totals[i] + jnp.sum(weight, axis=-1, keepdims=True)
                weighted[i] = weighted[i] + jnp.dot(
                    weight.astype(jnp.bfloat16),
                    pair[:, width + i * HD : width + (i + 1) * HD],
                    preferred_element_type=jnp.float32,
                )
        context = jnp.concatenate(
            [(weighted[i] / totals[i]).astype(jnp.bfloat16) for i in range(heads)], axis=1
        )
        partial = jnp.dot(context, wo[...], preferred_element_type=jnp.float32)
        part[place] = partial.astype(jnp.bfloat16).reshape(2, rows, partial.shape[1])

    rs = (rs_s, rs_r)
    a_send = send(part.at[0, other], got_a, rs, 0, dev_other)
    b_left = send(part.at[1, other], got_b.at[0], rs, 1, dev_left)
    b_right = send(part.at[2, other], got_b.at[1], rs, 2, dev_right)
    c_left_high = send(part.at[1, y, high], got_c.at[0, high], rs, 3, dev_left)
    c_left_low = send(part.at[1, y, low], got_c.at[0, low], rs, 4, dev_left)
    c_right_high = send(part.at[2, y, high], got_c.at[1, high], rs, 5, dev_right)
    c_right_low = send(part.at[2, y, low], got_c.at[1, low], rs, 6, dev_right)
    h_left = send(part.at[0, y, low], got_h.at[0], rs, 7, dev_left)
    h_right = send(part.at[0, y, high], got_h.at[1], rs, 8, dev_right)
    d_send = send(part.at[3, other], got_d, rs, 9, dev_other)

    def wide_sum(*terms):
        total = terms[0].astype(jnp.float32)
        for term in terms[1:]:
            total = total + term.astype(jnp.float32)
        return total.astype(jnp.bfloat16)

    attend(opposite, 0)
    a_send.start()
    attend(left, 1)
    b_left.start()
    c_left_high.start()
    attend(right, 2)
    b_right.start()
    c_right_low.start()
    attend(x, 3)

    a_send.wait_recv()
    part[0, y] = wide_sum(part[0, y], got_a[...])
    h_left.start()
    h_right.start()
    b_left.wait_recv()
    b_right.wait_recv()
    part[3, other] = wide_sum(part[3, other], got_b[0], got_b[1])
    d_send.start()
    h_left.wait_recv()
    part[1, y, 0:half] = wide_sum(part[1, y, 0:half], got_h[0])
    c_left_low.start()
    h_right.wait_recv()
    part[2, y, half:rows] = wide_sum(part[2, y, half:rows], got_h[1])
    c_right_high.start()
    for copy in (c_left_high, c_right_low, d_send, c_left_low, c_right_high):
        copy.wait_recv()
    out_ref[...] = wide_sum(part[3, y], got_c[0], got_c[1], got_d[...])

    for copy in (a_right, a_left, b_other, f_right, f_left, c_right, c_left, d_high, d_low):
        copy.wait_send()
    for i, d in enumerate(reach):

        @pl.when(within(d))
        def _():
            frame_copy(i, d).wait_send()

    for copy in (a_send, b_left, b_right, c_left_high, c_left_low, c_right_high, c_right_low):
        copy.wait_send()
    for copy in (h_left, h_right, d_send):
        copy.wait_send()


def per_device(
    tokens,
    norm_gain,
    w_query,
    w_key,
    w_value,
    query_gain,
    key_gain,
    w_out,
    block_lists,
    block_counts,
):
    rows, depth = tokens.shape
    width = w_query.shape[1]
    dma = pltpu.SemaphoreType.DMA
    bf16 = jnp.bfloat16
    vmem = pl.BlockSpec(memory_space=pltpu.VMEM)
    smem = pl.BlockSpec(memory_space=pltpu.SMEM)
    hbm = pl.BlockSpec(memory_space=pl.ANY)
    return pl.pallas_call(
        functools.partial(kernel, lax.axis_size("frame")),
        out_shape=jax.ShapeDtypeStruct((rows, depth), bf16),
        in_specs=[vmem, vmem, vmem, vmem, smem, smem, hbm, hbm, hbm, hbm],
        out_specs=vmem,
        scratch_shapes=[
            pltpu.VMEM((depth, width), bf16),
            pltpu.VMEM((depth, width), bf16),
            pltpu.VMEM((depth, width), bf16),
            pltpu.VMEM((width, depth), bf16),
            pltpu.VMEM((8, rows, depth), bf16),
            pltpu.VMEM((8, rows, width), bf16),
            pltpu.VMEM(((2 * BAND + 1) * 8, rows, 2 * width), bf16),
            pltpu.VMEM((4, 2, rows, depth), bf16),
            pltpu.VMEM((rows, depth), bf16),
            pltpu.VMEM((2, rows // 2, depth), bf16),
            pltpu.VMEM((2, rows, depth), bf16),
            pltpu.VMEM((2, rows, depth), bf16),
            pltpu.VMEM((rows, depth), bf16),
            dma((4,)),
            dma((9,)),
            dma((9,)),
            dma((2 * BAND,)),
            dma((2 * BAND,)),
            dma((10,)),
            dma((10,)),
        ],
        compiler_params=pltpu.CompilerParams(
            collective_id=0, has_side_effects=True, vmem_limit_bytes=48 * 1024 * 1024
        ),
    )(
        tokens,
        norm_gain.reshape(1, depth),
        query_gain.reshape(1, HD),
        key_gain.reshape(1, HD),
        block_lists,
        block_counts,
        w_query,
        w_key,
        w_value,
        w_out,
    )


def solution(mesh):
    placed = (
        P(("frame", "head"), None),
        P(),
        P(None, "head"),
        P(None, "head"),
        P(None, "head"),
        P(),
        P(),
        P("head", None),
        P("frame", None),
        P("frame"),
    )
    return jax.shard_map(
        per_device,
        mesh=mesh,
        in_specs=placed,
        out_specs=P(("frame", "head"), None),
        check_vma=False,
    )
```

time: 619 us -> 90.3 us (0.15)
  the two profiles are of different devices: /device:TPU:16 before, /device:TPU:40 now
where the time goes in v1:
time: 90.3 us; the launch traced here: 89.9 us
  Pallas kernels  80.6 us (89%)
  local copies, waits for them, and re-layouts  9.32 us (10%)
    pallas_call x1, Pallas kernels, per_device(): pl.pallas_call(functools.partial(kernel, lax.axis_size('frame')), out_sha...  80.6 us
    unnamed x19, local copies, waits for them, and re-layouts  9.32 us

profile of v1, /device:TPU:40, one launch (start us, length us, event | category | flops | bytes accessed | tf_op | source)
XLA Modules:
  0.0 89.9 jit_solution(10682132303683611231)
XLA Ops:
  0.0 0.0 copy-start
  0.0 1.4 %copy-done = bf16[3072,256]{1,0:T(8,128)(2,1)S(1)} copy-done((bf16[3072,256]{1,0:T(8,128)(2,1)S(1)}, bf16[3072,256]{1,0:T(8,128)(2,1)}, u32[]{:S(2)}) %copy-start) | copy-done | bytes 1572888
  1.4 0.0 copy-start.1
  1.4 1.4 %copy-done.1 = bf16[3072,256]{1,0:T(8,128)(2,1)S(1)} copy-done((bf16[3072,256]{1,0:T(8,128)(2,1)S(1)}, bf16[3072,256]{1,0:T(8,128)(2,1)}, u32[]{:S(2)}) %copy-start.1) | copy-done | bytes 1572888
  2.8 0.0 copy-start.2
  2.8 1.4 %copy-done.2 = bf16[3072,256]{1,0:T(8,128)(2,1)S(1)} copy-done((bf16[3072,256]{1,0:T(8,128)(2,1)S(1)}, bf16[3072,256]{1,0:T(8,128)(2,1)}, u32[]{:S(2)}) %copy-start.2) | copy-done | bytes 1572888
  4.2 0.0 copy-start.3
  4.2 1.0 %copy-done.3 = bf16[64,3072]{1,0:T(8,128)(2,1)S(1)} copy-done((bf16[64,3072]{1,0:T(8,128)(2,1)S(1)}, bf16[64,3072]{1,0:T(8,128)(2,1)}, u32[]{:S(2)}) %copy-start.3) | copy-done | bytes 393240
  5.2 0.0 copy-start.4
  5.2 0.7 copy-done.4
  5.9 0.0 copy-start.5
  5.9 0.7 copy-done.5
  6.6 0.0 copy-start.6
  6.6 0.7 copy-done.6
  7.3 0.0 copy-start.7
  7.3 0.7 copy-done.7
  7.9 0.0 copy-start.8
  7.9 0.7 copy-done.8
  8.6 80.6 %shard_map.100 = bf16[64,3072]{1,0:T(8,128)(2,1)S(1)} custom-call(bf16[64,3072]{1,0:T(8,128)(2,1)S(1)} %copy-done.3, f32[1,3072]{1,0:T(1,128)S(1)} %bitcast.3, f32[1,128]{1,0:T(1,128)S(1)} %bitcast.4, f32[1,128]{1,0:T(1,128)S(1)} %bitcast.5, s32[4,6]{1,0:T(4,128)S(1)} %copy-done.5, s32[4]{0:T(128)S(1)} %copy-done.8, bf16[3072,256]{1,0:T(8,128)(2,1)S(1)} %copy-done, ...), custom_call_target="tpu_custom_call" | custom-call | tf_op jit(solution)/shard_map/pallas_call | solution.py:316
  89.2 0.7 copy.12
Async XLA Ops:
  0.0 1.4 %copy-start = (bf16[3072,256]{1,0:T(8,128)(2,1)S(1)}, bf16[3072,256]{1,0:T(8,128)(2,1)}, u32[]{:S(2)}) copy-start(bf16[3072,256]{1,0:T(8,128)(2,1)} %wq_hbm.1) | copy-start | bytes 4718596
  1.4 1.4 %copy-start.1 = (bf16[3072,256]{1,0:T(8,128)(2,1)S(1)}, bf16[3072,256]{1,0:T(8,128)(2,1)}, u32[]{:S(2)}) copy-start(bf16[3072,256]{1,0:T(8,128)(2,1)} %wk_hbm.1) | copy-start | bytes 4718596
  2.8 1.4 %copy-start.2 = (bf16[3072,256]{1,0:T(8,128)(2,1)S(1)}, bf16[3072,256]{1,0:T(8,128)(2,1)}, u32[]{:S(2)}) copy-start(bf16[3072,256]{1,0:T(8,128)(2,1)} %wv_hbm.1) | copy-start | bytes 4718596
  4.2 1.0 %copy-start.3 = (bf16[64,3072]{1,0:T(8,128)(2,1)S(1)}, bf16[64,3072]{1,0:T(8,128)(2,1)}, u32[]{:S(2)}) copy-start(bf16[64,3072]{1,0:T(8,128)(2,1)} %tokens_ref.1) | copy-start | bytes 1179652
  5.2 0.7 copy-start.4
  5.9 0.7 copy-start.5
  6.6 0.7 copy-start.6
  7.3 0.7 copy-start.7
  7.9 0.7 copy-start.8

commit v2 on v1

v2 whole, which is shorter than its diff:
```python
import functools

import jax
import jax.numpy as jnp
from jax import lax
from jax.experimental import pallas as pl
from jax.experimental.pallas import tpu as pltpu
from jax.sharding import PartitionSpec as P

HD = 128
BLK = 128
MAXB = 6
BAND = 2
NB = 4
EPS = 1e-06
PIECES = 4
MESH = pl.DeviceIdType.MESH

PLACE = (0, 1, 6, 2, 4, 7, 3, 5)


def kernel(
    frames,
    tokens_hbm,
    ngain_hbm,
    qgain_hbm,
    kgain_hbm,
    lists_hbm,
    counts_hbm,
    wq_hbm,
    wk_hbm,
    wv_hbm,
    wo_hbm,
    out_ref,
    tokens_ref,
    ngain_ref,
    qgain_ref,
    kgain_ref,
    lists_ref,
    counts_ref,
    wq,
    wk,
    wv,
    wo,
    xn,
    q,
    kv,
    ctx,
    part,
    got_h,
    got_c,
    in_sem,
    ag_s,
    ag_r,
    kv_s,
    kv_r,
    wo_s,
    wo_r,
    ctx_s,
    ctx_r,
    rs_s,
    rs_r,
):
    f = lax.axis_index("frame")
    head = lax.axis_index("head")
    x, y = head // 2, head % 2
    core = f % 2
    toward = 1 - 2 * core
    right, left = (x + 1) % 4, (x + 3) % 4
    to_right, to_left = {"head": right * 2 + y}, {"head": left * 2 + y}
    to_other = {"head": x * 2 + 1 - y}
    to_sibling = {"frame": f + toward}
    to_far = {"frame": f + 2 * toward}
    to_near = {"frame": f - toward}
    to_across = {"frame": (f + frames // 2) % frames, "head": x * 2 + 1 - y}
    rows = tokens_ref.shape[0]
    half, piece = rows // 2, rows // PIECES
    width = wq.shape[1]
    heads = width // HD

    def within(d):
        return jnp.logical_and(f + d >= 0, f + d < frames)

    far_to, far_from, near = within(2 * toward), within(-2 * toward), within(-toward)

    loads = [
        pltpu.make_async_copy(src, dst, in_sem.at[i])
        for i, (src, dst) in enumerate(
            (
                (tokens_hbm, tokens_ref),
                (ngain_hbm, ngain_ref),
                (qgain_hbm, qgain_ref),
                (kgain_hbm, kgain_ref),
                (lists_hbm, lists_ref),
                (counts_hbm, counts_ref),
                (wk_hbm, wk),
                (wv_hbm, wv),
                (wq_hbm, wq),
                (wo_hbm, wo.at[0:width]),
            )
        )
    ]
    for copy in loads:
        copy.start()

    barrier = pltpu.get_barrier_semaphore()

    def greet(device):
        pl.semaphore_signal(barrier, inc=1, device_id=device, device_id_type=MESH)

    for device in (to_right, to_left, to_other, to_sibling, to_across):
        greet(device)
    peers = 5
    for there, device in (
        (far_to, to_far),
        (far_from, {"frame": f - 2 * toward}),
        (near, to_near),
    ):
        pl.when(there)(functools.partial(greet, device))
        peers = peers + jnp.where(there, 1, 0)

    loads[0].wait()
    loads[1].wait()
    wide = tokens_ref[...].astype(jnp.float32)
    factor = lax.rsqrt(jnp.mean(wide * wide, axis=-1, keepdims=True) + EPS)
    xn[0] = (wide * factor * ngain_ref[...]).astype(jnp.bfloat16)

    pl.semaphore_wait(barrier, peers)

    sent = []

    def send(src, dst, sems, index, device, keep=True):
        copy = pltpu.make_async_remote_copy(
            src_ref=src,
            dst_ref=dst,
            send_sem=sems[0].at[index],
            recv_sem=sems[1].at[index],
            device_id=device,
            device_id_type=MESH,
        )
        if keep:
            sent.append(copy)
        return copy

    def rows_of(p):
        return pl.ds(p * piece, piece)

    ag = (ag_s, ag_r)
    a_right, a_left, b_other, f_ward, c_right, c_left, d_other = [], [], [], [], [], [], []
    for p in range(PIECES):
        r = rows_of(p)
        n = 7 * p
        a_right.append(send(xn.at[0, r], xn.at[2, r], ag, n, to_right))
        a_left.append(send(xn.at[0, r], xn.at[3, r], ag, n + 1, to_left))
        b_other.append(send(xn.at[0, r], xn.at[1, r], ag, n + 2, to_other))
        if p % 2:
            f_ward.append(send(xn.at[2, r], xn.at[4, r], ag, n + 3, to_right))
        else:
            f_ward.append(send(xn.at[3, r], xn.at[4, r], ag, n + 3, to_left))
        c_right.append(send(xn.at[1, r], xn.at[5, r], ag, n + 4, to_right))
        c_left.append(send(xn.at[1, r], xn.at[6, r], ag, n + 5, to_left))
        d_other.append(send(xn.at[4, r], xn.at[7, r], ag, n + 6, to_other))

    def normed_heads(section, gain_ref):
        done = []
        for i in range(heads):
            part_i = section[:, i * HD : (i + 1) * HD]
            scale = lax.rsqrt(jnp.mean(part_i * part_i, axis=-1, keepdims=True) + EPS)
            done.append((part_i * scale * gain_ref[...]).astype(jnp.bfloat16))
        return done

    groups = (
        ((0,), 0, rows, 0),
        ((1, 2, 3), 0, rows, 1),
        ((4,), 0, rows, 4),
        ((5, 6, 7), 0, half, 5),
        ((5, 6, 7), half, half, 8),
    )
    kinds = 4
    copies = 11

    def gathered(group):
        slots, low, count, _ = group
        block = xn[slots[0] : slots[-1] + 1, low : low + count]
        return block.reshape(len(slots) * count, block.shape[-1])

    def kv_copies(group, kind):
        slots, low, count, first = group
        into = (BAND - toward, BAND - 2 * toward, BAND + toward, BAND - 2 * toward)[kind]
        out = BAND - toward if kind == 3 else BAND
        device = (to_sibling, to_far, to_near, to_sibling)[kind]
        r = pl.ds(low, count)
        return [
            send(
                kv.at[out * 8 + PLACE[slot], r],
                kv.at[into * 8 + PLACE[slot], r],
                (kv_s, kv_r),
                kind * copies + first + i,
                device,
                keep=False,
            )
            for i, slot in enumerate(slots)
        ]

    def start_all(some):
        for copy in some:
            copy.start()

    def project_pairs(group):
        slots, low, count, _ = group
        block = gathered(group)
        keys = jnp.dot(block, wk[...], preferred_element_type=jnp.float32)
        pieces = normed_heads(keys, kgain_ref)
        values = jnp.dot(block, wv[...], preferred_element_type=jnp.float32).astype(jnp.bfloat16)
        for n, slot in enumerate(slots):
            at = BAND * 8 + PLACE[slot]
            for i in range(heads):
                kv[at, low : low + count, i * HD : (i + 1) * HD] = pieces[i][
                    n * count : (n + 1) * count
                ]
            kv[at, low : low + count, width:] = values[n * count : (n + 1) * count]
        start_all(kv_copies(group, 0))
        pl.when(far_to)(lambda: start_all(kv_copies(group, 1)))
        pl.when(near)(lambda: start_all(kv_copies(group, 2)))

    def project_queries(group):
        slots, low, count, _ = group
        queries = jnp.dot(gathered(group), wq[...], preferred_element_type=jnp.float32)
        pieces = normed_heads(queries, qgain_ref)
        for n, slot in enumerate(slots):
            for i in range(heads):
                q[PLACE[slot], low : low + count, i * HD : (i + 1) * HD] = pieces[i][
                    n * count : (n + 1) * count
                ]

    def relay(group):
        @pl.when(near)
        def _():
            for came, on in zip(kv_copies(group, 2), kv_copies(group, 3)):
                came.wait_recv()
                on.start()

    for p in range(PIECES):
        a_right[(1, 3, 0, 2)[p]].start()
        a_left[p if p in (0, 3) else 3 - p].start()
        b_other[p].start()

    share = width // 2
    wo_send = send(
        wo_hbm.at[pl.ds(core * share, share)],
        wo.at[pl.ds(width + core * share, share)],
        (wo_s, wo_r),
        0,
        to_across,
    )
    wo_pass = send(
        wo.at[pl.ds(width + core * share, share)],
        wo.at[pl.ds(width + core * share, share)],
        (wo_s, wo_r),
        1,
        to_sibling,
    )
    wo_send.start()

    for copy in loads[2:8]:
        copy.wait()
    project_pairs(groups[0])
    loads[8].wait()
    project_queries(groups[0])

    for early, late in ((0, 1), (2, 3)):
        a_right[late].wait_recv()
        f_ward[late].start()
        a_left[early].wait_recv()
        f_ward[early].start()
        for p in (early, late):
            b_other[p].wait_recv()
            c_right[p].start()
            c_left[p].start()
    for p in (0, 2):
        a_right[p].wait_recv()
        a_left[p + 1].wait_recv()
    project_pairs(groups[1])
    relay(groups[0])
    for p in range(PIECES):
        f_ward[p].wait_recv()
        d_other[p].start()
    project_queries(groups[1])
    project_pairs(groups[2])
    relay(groups[1])
    project_queries(groups[2])
    for late in range(2):
        for p in (2 * late, 2 * late + 1):
            c_right[p].wait_recv()
            c_left[p].wait_recv()
            d_other[p].wait_recv()
        project_pairs(groups[3 + late])
        relay(groups[2 + late])
        project_queries(groups[3 + late])
    loads[9].wait()
    wo_send.wait_recv()
    wo_pass.start()
    relay(groups[4])

    for group in groups:
        for copy in kv_copies(group, 0):
            copy.wait_recv()

        @pl.when(far_from)
        def _():
            for copy in kv_copies(group, 1):
                copy.wait_recv()

        @pl.when(far_to)
        def _():
            for copy in kv_copies(group, 3):
                copy.wait_recv()

    score_factor = 1.0 / HD**0.5

    def attend(k):
        block = (x + k) % 4
        queries = q[2 * k : 2 * k + 2].reshape(BLK, width)
        listed = counts_ref[block]
        weighted = [jnp.zeros((BLK, HD), jnp.float32) for _ in range(heads)]
        totals = [jnp.zeros((BLK, 1), jnp.float32) for _ in range(heads)]
        for m in range(MAXB):
            live = m < listed
            picked = jnp.where(live, lists_ref[block, m], f * NB + block)
            slot = jnp.clip(picked // NB - f + BAND, 0, 2 * BAND)
            spot = slot * NB + (picked % NB - x + 4) % 4
            pair = kv[pl.ds(spot * 2, 2)].reshape(BLK, 2 * width)
            on = jnp.where(live, 1.0, 0.0).astype(jnp.float32)
            for i in range(heads):
                scores = lax.dot_general(
                    queries[:, i * HD : (i + 1) * HD],
                    pair[:, i * HD : (i + 1) * HD],
                    (((1,), (1,)), ((), ())),
                    preferred_element_type=jnp.float32,
                )
                weight = jnp.exp(scores * score_factor) * on
                totals[i] = totals[i] + jnp.sum(weight, axis=-1, keepdims=True)
                weighted[i] = weighted[i] + jnp.dot(
                    weight.astype(jnp.bfloat16),
                    pair[:, width + i * HD : width + (i + 1) * HD],
                    preferred_element_type=jnp.float32,
                )
        for i in range(heads):
            done = (weighted[i] / totals[i]).astype(jnp.bfloat16)
            ctx[k, 0, :, i * HD : (i + 1) * HD] = done[0:rows]
            ctx[k, 1, :, i * HD : (i + 1) * HD] = done[rows:]

    ctx_sends = [
        send(ctx.at[k, 1], ctx.at[k, 2], (ctx_s, ctx_r), k, to_other) for k in range(4)
    ]

    def out_project(k):
        partial = jnp.dot(ctx[k, 0], wo[0:width], preferred_element_type=jnp.float32)
        partial = partial + jnp.dot(ctx[k, 2], wo[width:], preferred_element_type=jnp.float32)
        part[k] = partial.astype(jnp.bfloat16)

    rs = (rs_s, rs_r)
    h_left, h_right, c_l, c_r = [], [], [], []
    for p in range(PIECES):
        r = rows_of(p)
        if p < PIECES // 2:
            h_left.append(send(part.at[2, r], got_h.at[r], rs, 3 * p, to_left))
        else:
            h_right.append(send(part.at[2, r], got_h.at[r], rs, 3 * p, to_right))
        c_l.append(send(part.at[3, r], got_c.at[0, r], rs, 3 * p + 1, to_left))
        c_r.append(send(part.at[1, r], got_c.at[1, r], rs, 3 * p + 2, to_right))

    for k in (2, 3, 1, 0):
        attend(k)
        ctx_sends[k].start()

    wo_pass.wait_recv()
    ctx_sends[2].wait_recv()
    out_project(2)
    for p in range(2):
        h_left[p].start()
        h_right[p].start()
    ctx_sends[3].wait_recv()
    out_project(3)
    c_l[2].start()
    c_l[3].start()
    ctx_sends[1].wait_recv()
    out_project(1)
    c_r[0].start()
    c_r[1].start()
    ctx_sends[0].wait_recv()
    out_project(0)

    def add_in(k, p):
        r = slice(p * piece, (p + 1) * piece)
        total = part[k, r].astype(jnp.float32) + got_h[r].astype(jnp.float32)
        part[k, r] = total.astype(jnp.bfloat16)

    for p in range(2):
        h_left[p].wait_recv()
        add_in(3, p)
        c_l[p].start()
        h_right[p].wait_recv()
        add_in(1, p + 2)
        c_r[p + 2].start()
    for p in (2, 3, 0, 1):
        r = slice(p * piece, (p + 1) * piece)
        c_l[p].wait_recv()
        c_r[(p + 2) % 4].wait_recv()
    total = part[0].astype(jnp.float32) + got_c[0].astype(jnp.float32)
    out_ref[...] = (total + got_c[1].astype(jnp.float32)).astype(jnp.bfloat16)

    for copy in sent:
        copy.wait_send()
    for kind, there in enumerate((None, far_to, near, near)):

        def finish():
            for group in groups:
                for copy in kv_copies(group, kind):
                    copy.wait_send()

        if there is None:
            finish()
        else:
            pl.when(there)(finish)


def per_device(
    tokens,
    norm_gain,
    w_query,
    w_key,
    w_value,
    query_gain,
    key_gain,
    w_out,
    block_lists,
    block_counts,
):
    rows, depth = tokens.shape
    width = w_query.shape[1]
    dma = pltpu.SemaphoreType.DMA
    bf16 = jnp.bfloat16
    hbm = pl.BlockSpec(memory_space=pltpu.HBM)
    return pl.pallas_call(
        functools.partial(kernel, lax.axis_size("frame")),
        out_shape=jax.ShapeDtypeStruct((rows, depth), bf16),
        in_specs=[hbm] * 10,
        out_specs=pl.BlockSpec(memory_space=pltpu.VMEM),
        scratch_shapes=[
            pltpu.VMEM((rows, depth), bf16),
            pltpu.VMEM((1, depth), jnp.float32),
            pltpu.VMEM((1, HD), jnp.float32),
            pltpu.VMEM((1, HD), jnp.float32),
            pltpu.SMEM(block_lists.shape, jnp.int32),
            pltpu.SMEM(block_counts.shape, jnp.int32),
            pltpu.VMEM((depth, width), bf16),
            pltpu.VMEM((depth, width), bf16),
            pltpu.VMEM((depth, width), bf16),
            pltpu.VMEM((2 * width, depth), bf16),
            pltpu.VMEM((8, rows, depth), bf16),
            pltpu.VMEM((8, rows, width), bf16),
            pltpu.VMEM(((2 * BAND + 1) * 8, rows, 2 * width), bf16),
            pltpu.VMEM((4, 3, rows, width), bf16),
            pltpu.VMEM((4, rows, depth), bf16),
            pltpu.VMEM((rows, depth), bf16),
            pltpu.VMEM((2, rows, depth), bf16),
            dma((10,)),
            dma((7 * PIECES,)),
            dma((7 * PIECES,)),
            dma((44,)),
            dma((44,)),
            dma((2,)),
            dma((2,)),
            dma((4,)),
            dma((4,)),
            dma((3 * PIECES,)),
            dma((3 * PIECES,)),
        ],
        compiler_params=pltpu.CompilerParams(
            collective_id=0, has_side_effects=True, vmem_limit_bytes=63 * 1024 * 1024
        ),
    )(
        tokens,
        norm_gain.reshape(1, depth),
        query_gain.reshape(1, HD),
        key_gain.reshape(1, HD),
        block_lists,
        block_counts,
        w_query,
        w_key,
        w_value,
        w_out,
    )


def solution(mesh):
    placed = (
        P(("frame", "head"), None),
        P(),
        P(None, "head"),
        P(None, "head"),
        P(None, "head"),
        P(),
        P(),
        P("head", None),
        P("frame", None),
        P("frame"),
    )
    return jax.shard_map(
        per_device,
        mesh=mesh,
        in_specs=placed,
        out_specs=P(("frame", "head"), None),
        check_vma=False,
    )
```

time: 90.3 us -> 64.3 us (0.71)
  the two profiles are of different devices: /device:TPU:40 before, /device:TPU:16 now
where the time goes in v2:
time: 64.3 us; the launch traced here: 64.2 us
  Pallas kernels  62.4 us (97%)
  local copies, waits for them, and re-layouts  1.77 us (3%)
    pallas_call x1, Pallas kernels, per_device(): pl.pallas_call(functools.partial(kernel, lax.axis_size('frame')), out_sha...  62.4 us
    unnamed x1, local copies, waits for them, and re-layouts  1.77 us

profile of v2, /device:TPU:16, one launch (start us, length us, event | category | flops | bytes accessed | tf_op | source)
XLA Modules:
  0.0 64.2 jit_solution(5554905543245087937)
XLA Ops:
  0.0 62.4 %shard_map.100 = bf16[64,3072]{1,0:T(8,128)(2,1)} custom-call(bf16[64,3072]{1,0:T(8,128)(2,1)} %tokens_hbm.1, f32[1,3072]{1,0:T(1,128)} %bitcast.3, f32[1,128]{1,0:T(1,128)} %bitcast.4, f32[1,128]{1,0:T(1,128)} %bitcast.5, s32[4,6]{1,0:T(4,128)} %lists_hbm.1, s32[4]{0:T(128)} %counts_hbm.1, bf16[3072,256]{1,0:T(8,128)(2,1)} %wq_hbm.1, ...), custom_call_target="tpu_custom_call" | custom-call | tf_op jit(solution)/shard_map/pallas_call | solution.py:445
  62.4 1.8 %copy.12 = bf16[64,3072]{1,0:T(8,128)(2,1)} copy(bf16[64,3072]{1,0:T(8,128)(2,1)} %shard_map.100) | data formatting | bytes 786432

commit v3 on v2

v3 whole, which is shorter than its diff:
```python
import functools

import jax
import jax.numpy as jnp
from jax import lax
from jax.experimental import pallas as pl
from jax.experimental.pallas import tpu as pltpu
from jax.sharding import PartitionSpec as P

HD = 128
BLK = 128
MAXB = 6
BAND = 2
NB = 4
EPS = 1e-06
PIECES = 4
MESH = pl.DeviceIdType.MESH

SLOT = (0, 2, 1, 3)


def kernel(
    frames,
    tokens_hbm,
    ngain_hbm,
    qgain_hbm,
    kgain_hbm,
    lists_hbm,
    counts_hbm,
    wq_hbm,
    wk_hbm,
    wv_hbm,
    wo_hbm,
    own_hbm,
    from_right_hbm,
    from_left_hbm,
    tokens_ref,
    ngain_ref,
    qgain_ref,
    kgain_ref,
    lists_ref,
    counts_ref,
    wq,
    wk,
    wv,
    wo,
    xn,
    q,
    kv,
    ctx,
    part,
    got_h,
    in_sem,
    ag_s,
    ag_r,
    kv_s,
    kv_r,
    wo_s,
    wo_r,
    ctx_s,
    ctx_r,
    rs_s,
    rs_r,
):
    f = lax.axis_index("frame")
    head = lax.axis_index("head")
    x, y = head // 2, head % 2
    core = f % 2
    toward = 1 - 2 * core
    right, left = (x + 1) % 4, (x + 3) % 4
    to_right, to_left = {"head": right * 2 + y}, {"head": left * 2 + y}
    to_other = {"head": x * 2 + 1 - y}
    to_sibling = {"frame": f + toward}
    to_far = {"frame": f + 2 * toward}
    to_near = {"frame": f - toward}
    to_across = {"frame": (f + frames // 2) % frames, "head": x * 2 + 1 - y}
    rows = tokens_ref.shape[0]
    half, piece = rows // 2, rows // PIECES
    width = wq.shape[1]
    heads = width // HD

    def within(d):
        return jnp.logical_and(f + d >= 0, f + d < frames)

    far_to, far_from, near = within(2 * toward), within(-2 * toward), within(-toward)
    mid = frames // 2
    crossing = jnp.logical_or(
        jnp.logical_and(f == mid - 1, core == 1), jnp.logical_and(f == mid, core == 0)
    )
    close = jnp.logical_and(near, jnp.logical_not(crossing))
    by_way = jnp.logical_not(far_to)
    to_way = {"frame": f - toward * (mid - 1)}
    from_way = {"frame": f + toward * (mid - 2)}
    to_crossing = {"frame": f - toward * (mid - 2)}

    loads = [
        pltpu.make_async_copy(src, dst, in_sem.at[i])
        for i, (src, dst) in enumerate(
            (
                (tokens_hbm, tokens_ref),
                (ngain_hbm, ngain_ref),
                (qgain_hbm, qgain_ref),
                (kgain_hbm, kgain_ref),
                (lists_hbm, lists_ref),
                (counts_hbm, counts_ref),
                (wk_hbm, wk),
                (wv_hbm, wv),
                (wq_hbm, wq),
                (wo_hbm, wo.at[0:width]),
            )
        )
    ]
    loads[0].start()
    loads[1].start()

    barrier = pltpu.get_barrier_semaphore()

    def greet(device):
        pl.semaphore_signal(barrier, inc=1, device_id=device, device_id_type=MESH)

    for device in (to_right, to_left, to_other, to_sibling, to_across):
        greet(device)
    peers = 5
    for there, device in (
        (far_to, to_far),
        (far_from, {"frame": f - 2 * toward}),
        (close, to_near),
        (crossing, to_way),
        (crossing, from_way),
        (by_way, to_way),
        (by_way, to_crossing),
    ):
        pl.when(there)(functools.partial(greet, device))
        peers = peers + jnp.where(there, 1, 0)

    loads[0].wait()
    loads[1].wait()
    for copy in loads[2:]:
        copy.start()
    wide = tokens_ref[...].astype(jnp.float32)
    factor = lax.rsqrt(jnp.mean(wide * wide, axis=-1, keepdims=True) + EPS)
    xn[0] = (wide * factor * ngain_ref[...]).astype(jnp.bfloat16)

    pl.semaphore_wait(barrier, peers)

    sent = []

    def send(src, dst, sems, index, device, keep=True):
        copy = pltpu.make_async_remote_copy(
            src_ref=src,
            dst_ref=dst,
            send_sem=sems[0].at[index],
            recv_sem=sems[1].at[index],
            device_id=device,
            device_id_type=MESH,
        )
        if keep:
            sent.append(copy)
        return copy

    def rows_of(p):
        return pl.ds(p * piece, piece)

    ag = (ag_s, ag_r)
    a_right, a_left, b_other, f_ward, c_right, c_left, d_other = [], [], [], [], [], [], []
    for p in range(PIECES):
        r = rows_of(p)
        n = 7 * p
        a_right.append(send(xn.at[0, r], xn.at[3, r], ag, n, to_right))
        a_left.append(send(xn.at[0, r], xn.at[2, r], ag, n + 1, to_left))
        b_other.append(send(xn.at[0, r], xn.at[4, r], ag, n + 2, to_other))
        if p % 2:
            f_ward.append(send(xn.at[3, r], xn.at[1, r], ag, n + 3, to_right))
        else:
            f_ward.append(send(xn.at[2, r], xn.at[1, r], ag, n + 3, to_left))
        c_right.append(send(xn.at[4, r], xn.at[7, r], ag, n + 4, to_right))
        c_left.append(send(xn.at[4, r], xn.at[6, r], ag, n + 5, to_left))
        d_other.append(send(xn.at[1, r], xn.at[5, r], ag, n + 6, to_other))

    def normed_heads(section, gain_ref):
        done = []
        for i in range(heads):
            part_i = section[:, i * HD : (i + 1) * HD]
            scale = lax.rsqrt(jnp.mean(part_i * part_i, axis=-1, keepdims=True) + EPS)
            done.append((part_i * scale * gain_ref[...]).astype(jnp.bfloat16))
        return done

    groups = (
        (0, 1, 0, rows),
        (2, 3, 0, rows),
        (1, 1, 0, rows),
        (5, 3, 0, half),
        (5, 3, half, piece),
        (5, 3, half + piece, piece),
    )

    def gathered(group):
        slot, count, low, each = groups[group]
        block = xn[slot : slot + count, low : low + each]
        return block.reshape(count * each, block.shape[-1])

    def kv_copy(group, kind):
        slot, count, low, each = groups[group]
        out, into, device, send_kind, recv_kind = (
            (BAND, BAND - toward, to_sibling, 0, 0),
            (BAND, BAND - 2 * toward, to_far, 1, 1),
            (BAND, BAND + toward, to_near, 2, 2),
            (BAND - toward, BAND - 2 * toward, to_sibling, 3, 3),
            (BAND, BAND - 2 * toward, to_way, 2, 3),
            (BAND + 2 * toward, BAND - toward, to_crossing, 1, 2),
        )[kind]
        r = pl.ds(low, each)
        return pltpu.make_async_remote_copy(
            src_ref=kv.at[pl.ds(out * 8 + slot, count), r],
            dst_ref=kv.at[pl.ds(into * 8 + slot, count), r],
            send_sem=kv_s.at[send_kind * len(groups) + group],
            recv_sem=kv_r.at[recv_kind * len(groups) + group],
            device_id=device,
            device_id_type=MESH,
        )

    def project_pairs(group):
        slot, count, low, each = groups[group]
        block = gathered(group)
        keys = jnp.dot(block, wk[...], preferred_element_type=jnp.float32)
        pieces = normed_heads(keys, kgain_ref)
        values = jnp.dot(block, wv[...], preferred_element_type=jnp.float32).astype(jnp.bfloat16)
        for n in range(count):
            at, r = BAND * 8 + slot + n, slice(n * each, (n + 1) * each)
            for i in range(heads):
                kv[at, low : low + each, i * HD : (i + 1) * HD] = pieces[i][r]
            kv[at, low : low + each, width:] = values[r]
        pl.when(close)(lambda: kv_copy(group, 2).start())
        pl.when(crossing)(lambda: kv_copy(group, 4).start())
        pl.when(far_to)(lambda: kv_copy(group, 1).start())
        kv_copy(group, 0).start()

    def project_queries(group):
        slot, count, low, each = groups[group]
        queries = jnp.dot(gathered(group), wq[...], preferred_element_type=jnp.float32)
        pieces = normed_heads(queries, qgain_ref)
        for n in range(count):
            for i in range(heads):
                q[slot + n, low : low + each, i * HD : (i + 1) * HD] = pieces[i][
                    n * each : (n + 1) * each
                ]

    def pass_on(group):
        @pl.when(by_way)
        def _():
            kv_copy(group, 3).wait_recv()
            kv_copy(group, 5).start()

    def relay(group):
        @pl.when(near)
        def _():
            kv_copy(group, 2).wait_recv()
            kv_copy(group, 3).start()

    for p in range(PIECES):
        a_right[(1, 3, 0, 2)[p]].start()
        a_left[p if p in (0, 3) else 3 - p].start()
        b_other[p].start()

    share = width // 2
    wo_send = send(
        wo_hbm.at[pl.ds(core * share, share)],
        wo.at[pl.ds(width + core * share, share)],
        (wo_s, wo_r),
        0,
        to_across,
    )
    wo_pass = send(
        wo.at[pl.ds(width + core * share, share)],
        wo.at[pl.ds(width + core * share, share)],
        (wo_s, wo_r),
        1,
        to_sibling,
    )
    wo_send.start()

    for copy in loads[2:8]:
        copy.wait()
    project_pairs(0)
    loads[8].wait()
    project_queries(0)

    for early, late in ((0, 1), (2, 3)):
        a_right[late].wait_recv()
        f_ward[late].start()
        a_left[early].wait_recv()
        f_ward[early].start()
        for p in (early, late):
            b_other[p].wait_recv()
            c_right[p].start()
            c_left[p].start()
    for p in (0, 2):
        a_right[p].wait_recv()
        a_left[p + 1].wait_recv()
    project_pairs(1)
    for p in range(PIECES):
        f_ward[p].wait_recv()
        d_other[p].start()
    pass_on(0)
    project_queries(1)
    project_pairs(2)
    relay(0)
    project_queries(2)
    pass_on(1)
    for first, last, group in ((0, 2, 3), (2, 3, 4), (3, 4, 5)):
        for p in range(first, last):
            c_right[p].wait_recv()
            c_left[p].wait_recv()
            d_other[p].wait_recv()
        project_pairs(group)
        pass_on(group - 1)
        if group < 5:
            project_queries(group)
            relay(group - 2)
    project_queries(5)
    loads[9].wait()
    wo_send.wait_recv()
    wo_pass.start()
    pass_on(5)
    for group in (3, 4, 5):
        relay(group)

    for group in range(len(groups)):
        kv_copy(group, 0).wait_recv()

        @pl.when(far_from)
        def _():
            kv_copy(group, 1).wait_recv()

        @pl.when(far_to)
        def _():
            kv_copy(group, 3).wait_recv()

    score_factor = 1.0 / HD**0.5

    def attend(k):
        block = (x + k) % 4
        own = SLOT[k]
        queries = jnp.concatenate([q[own], q[own + 4]], axis=0)
        listed = counts_ref[block]
        pairs, on = [], []
        for m in range(MAXB):
            live = m < listed
            picked = jnp.where(live, lists_ref[block, m], f * NB + block)
            frame = jnp.clip(picked // NB - f + BAND, 0, 2 * BAND)
            across = (picked % NB - x + 4) % 4
            spot = frame * 8 + (across % 2) * 2 + across // 2
            pairs += [kv[spot], kv[spot + 4]]
            on.append(jnp.where(live, 1.0, 0.0).astype(jnp.float32))
        weighted, totals = [], []
        for i in range(heads):
            keys = jnp.concatenate([pair[:, i * HD : (i + 1) * HD] for pair in pairs], axis=0)
            values = jnp.concatenate(
                [pair[:, width + i * HD : width + (i + 1) * HD] for pair in pairs], axis=0
            )
            scores = lax.dot_general(
                queries[:, i * HD : (i + 1) * HD],
                keys,
                (((1,), (1,)), ((), ())),
                preferred_element_type=jnp.float32,
            )
            weights = [
                jnp.exp(scores[:, m * BLK : (m + 1) * BLK] * score_factor) * on[m]
                for m in range(MAXB)
            ]
            summed = functools.reduce(jnp.add, weights)
            totals.append(jnp.sum(summed, axis=-1, keepdims=True))
            rounded = jnp.concatenate([weight.astype(jnp.bfloat16) for weight in weights], axis=1)
            weighted.append(jnp.dot(rounded, values, preferred_element_type=jnp.float32))
        for i in range(heads):
            done = (weighted[i] / totals[i]).astype(jnp.bfloat16)
            ctx[k, 0, :, i * HD : (i + 1) * HD] = done[0:rows]
            ctx[k, 1, :, i * HD : (i + 1) * HD] = done[rows:]

    ctx_sends = [
        send(ctx.at[k, 1], ctx.at[k, 2], (ctx_s, ctx_r), k, to_other) for k in range(4)
    ]

    def out_project(k):
        partial = jnp.dot(ctx[k, 0], wo[0:width], preferred_element_type=jnp.float32)
        partial = partial + jnp.dot(ctx[k, 2], wo[width:], preferred_element_type=jnp.float32)
        part[k] = partial.astype(jnp.bfloat16)

    rs = (rs_s, rs_r)
    h_left, h_right, c_l, c_r = [], [], [], []
    for p in range(PIECES):
        r = rows_of(p)
        if p < PIECES // 2:
            h_left.append(send(part.at[2, r], got_h.at[r], rs, 3 * p, to_left))
        else:
            h_right.append(send(part.at[2, r], got_h.at[r], rs, 3 * p, to_right))
        c_l.append(send(part.at[3, r], from_right_hbm.at[r], rs, 3 * p + 1, to_left))
        c_r.append(send(part.at[1, r], from_left_hbm.at[r], rs, 3 * p + 2, to_right))

    for k in (2, 3, 1):
        attend(k)
        ctx_sends[k].start()
    wo_pass.wait_recv()
    ctx_sends[2].wait_recv()
    out_project(2)
    for p in range(2):
        h_left[p].start()
        h_right[p].start()
    attend(0)
    ctx_sends[0].start()
    ctx_sends[3].wait_recv()
    out_project(3)
    c_l[2].start()
    c_l[3].start()
    ctx_sends[1].wait_recv()
    out_project(1)
    c_r[0].start()
    c_r[1].start()

    def add_in(k, p):
        r = slice(p * piece, (p + 1) * piece)
        total = part[k, r].astype(jnp.float32) + got_h[r].astype(jnp.float32)
        part[k, r] = total.astype(jnp.bfloat16)

    for p in range(2):
        h_left[p].wait_recv()
        add_in(3, p)
        c_l[p].start()
        h_right[p].wait_recv()
        add_in(1, p + 2)
        c_r[p + 2].start()
    ctx_sends[0].wait_recv()
    out_project(0)
    mine = pltpu.make_async_copy(part.at[0], own_hbm, in_sem.at[0])
    mine.start()
    for p in (2, 3, 0, 1):
        c_l[p].wait_recv()
        c_r[(p + 2) % 4].wait_recv()
    mine.wait()

    for copy in sent:
        copy.wait_send()
    for kind, there in ((0, None), (1, far_to), (2, close), (3, near), (4, crossing), (5, by_way)):

        def finish():
            for group in range(len(groups)):
                kv_copy(group, kind).wait_send()

        if there is None:
            finish()
        else:
            pl.when(there)(finish)


def per_device(
    tokens,
    norm_gain,
    w_query,
    w_key,
    w_value,
    query_gain,
    key_gain,
    w_out,
    block_lists,
    block_counts,
):
    rows, depth = tokens.shape
    width = w_query.shape[1]
    dma = pltpu.SemaphoreType.DMA
    bf16 = jnp.bfloat16
    hbm = pl.BlockSpec(memory_space=pltpu.HBM)
    terms = pl.pallas_call(
        functools.partial(kernel, lax.axis_size("frame")),
        out_shape=[jax.ShapeDtypeStruct((rows, depth), bf16)] * 3,
        in_specs=[hbm] * 10,
        out_specs=[hbm] * 3,
        scratch_shapes=[
            pltpu.VMEM((rows, depth), bf16),
            pltpu.VMEM((1, depth), jnp.float32),
            pltpu.VMEM((1, HD), jnp.float32),
            pltpu.VMEM((1, HD), jnp.float32),
            pltpu.SMEM(block_lists.shape, jnp.int32),
            pltpu.SMEM(block_counts.shape, jnp.int32),
            pltpu.VMEM((depth, width), bf16),
            pltpu.VMEM((depth, width), bf16),
            pltpu.VMEM((depth, width), bf16),
            pltpu.VMEM((2 * width, depth), bf16),
            pltpu.VMEM((8, rows, depth), bf16),
            pltpu.VMEM((8, rows, width), bf16),
            pltpu.VMEM(((2 * BAND + 1) * 8, rows, 2 * width), bf16),
            pltpu.VMEM((4, 3, rows, width), bf16),
            pltpu.VMEM((4, rows, depth), bf16),
            pltpu.VMEM((rows, depth), bf16),
            dma((10,)),
            dma((7 * PIECES,)),
            dma((7 * PIECES,)),
            dma((24,)),
            dma((24,)),
            dma((2,)),
            dma((2,)),
            dma((4,)),
            dma((4,)),
            dma((3 * PIECES,)),
            dma((3 * PIECES,)),
        ],
        compiler_params=pltpu.CompilerParams(
            collective_id=0, has_side_effects=True, vmem_limit_bytes=63 * 1024 * 1024
        ),
    )(
        tokens,
        norm_gain.reshape(1, depth),
        query_gain.reshape(1, HD),
        key_gain.reshape(1, HD),
        block_lists,
        block_counts,
        w_query,
        w_key,
        w_value,
        w_out,
    )
    own, from_right, from_left = (term.astype(jnp.float32) for term in terms)
    return (own + from_right + from_left).astype(bf16)


def solution(mesh):
    placed = (
        P(("frame", "head"), None),
        P(),
        P(None, "head"),
        P(None, "head"),
        P(None, "head"),
        P(),
        P(),
        P("head", None),
        P("frame", None),
        P("frame"),
    )
    return jax.shard_map(
        per_device,
        mesh=mesh,
        in_specs=placed,
        out_specs=P(("frame", "head"), None),
        check_vma=False,
    )
```

time: 64.3 us -> 67.3 us (1.047)
  Pallas kernels: 62.4 us -> 64.8 us
  other arithmetic: 0 us -> 2.12 us
  local copies, waits for them, and re-layouts: 1.77 us -> 0 us
    pallas_call x1, Pallas kernels: 62.4 us -> 64.8 us  [per_device(): pl.pallas_call(functools.partial(kernel, lax.axis_size('frame')), out_sha...]
    convert_element_type x0 -> x1, other arithmetic: none -> 2.12 us  [per_device(): return (own + from_right + from_left).astype(bf16)]
    unnamed x1 -> x0, local copies, waits for them, and re-layouts: 1.77 us -> none
where the time goes in v3:
time: 67.3 us; the launch traced here: 66.9 us
  Pallas kernels  64.8 us (96%)
  other arithmetic  2.12 us (3%)
    pallas_call x1, Pallas kernels, per_device(): pl.pallas_call(functools.partial(kernel, lax.axis_size('frame')), out_sha...  64.8 us
    convert_element_type x1, other arithmetic, per_device(): return (own + from_right + from_left).astype(bf16)  2.12 us

profile of v3, /device:TPU:16, one launch (start us, length us, event | category | flops | bytes accessed | tf_op | source)
XLA Modules:
  0.0 66.9 jit_solution(14476855513522392196)
XLA Ops:
  0.0 64.8 %shard_map.100 = (bf16[64,3072]{1,0:T(8,128)(2,1)}, bf16[64,3072]{1,0:T(8,128)(2,1)}, bf16[64,3072]{1,0:T(8,128)(2,1)}) custom-call(bf16[64,3072]{1,0:T(8,128)(2,1)} %tokens_hbm.1, f32[1,3072]{1,0:T(1,128)} %bitcast.3, f32[1,128]{1,0:T(1,128)} %bitcast.4, f32[1,128]{1,0:T(1,128)} %bitcast.5, s32[4,6]{1,0:T(4,128)} %lists_hbm.1, s32[4]{0:T(128)} %counts_hbm.1, ...), custom_call_target="tpu_custom_call" | custom-call | tf_op jit(solution)/shard_map/pallas_call | solution.py:472
  64.8 2.1 %add_convert_fusion = bf16[64,3072]{1,0:T(8,128)(2,1)} fusion(bf16[64,3072]{1,0:T(8,128)(2,1)} %get-tuple-element.10, bf16[64,3072]{1,0:T(8,128)(2,1)} %get-tuple-element.9, bf16[64,3072]{1,0:T(8,128)(2,1)} %get-tuple-element.8), kind=kLoop, calls=%fused_computation | loop fusion | flops 1179648 | bytes 1572864 | tf_op jit(solution)/shard_map/convert_element_type | solution.py:522

commit v4 on v3

--- a/solution.py
+++ b/solution.py
@@ -14,6 +14,7 @@
 NB = 4
 EPS = 1e-06
 PIECES = 4
+BY_WAY = 2
 MESH = pl.DeviceIdType.MESH
 
 SLOT = (0, 2, 1, 3)
@@ -124,7 +125,7 @@
     for there, device in (
         (far_to, to_far),
         (far_from, {"frame": f - 2 * toward}),
-        (close, to_near),
+        (near, to_near),
         (crossing, to_way),
         (crossing, from_way),
         (by_way, to_way),
@@ -230,8 +231,11 @@
             for i in range(heads):
                 kv[at, low : low + each, i * HD : (i + 1) * HD] = pieces[i][r]
             kv[at, low : low + each, width:] = values[r]
-        pl.when(close)(lambda: kv_copy(group, 2).start())
-        pl.when(crossing)(lambda: kv_copy(group, 4).start())
+        if group < BY_WAY:
+            pl.when(close)(lambda: kv_copy(group, 2).start())
+            pl.when(crossing)(lambda: kv_copy(group, 4).start())
+        else:
+            pl.when(near)(lambda: kv_copy(group, 2).start())
         pl.when(far_to)(lambda: kv_copy(group, 1).start())
         kv_copy(group, 0).start()
 
@@ -251,8 +255,8 @@
             kv_copy(group, 3).wait_recv()
             kv_copy(group, 5).start()
 
-    def relay(group):
-        @pl.when(near)
+    def relay(group, there):
+        @pl.when(there)
         def _():
             kv_copy(group, 2).wait_recv()
             kv_copy(group, 3).start()
@@ -304,26 +308,27 @@
     pass_on(0)
     project_queries(1)
     project_pairs(2)
-    relay(0)
     project_queries(2)
-    pass_on(1)
+    relay(0, close)
     for first, last, group in ((0, 2, 3), (2, 3, 4), (3, 4, 5)):
         for p in range(first, last):
             c_right[p].wait_recv()
             c_left[p].wait_recv()
             d_other[p].wait_recv()
         project_pairs(group)
-        pass_on(group - 1)
+        if group - 2 < BY_WAY:
+            pass_on(group - 2)
         if group < 5:
             project_queries(group)
-            relay(group - 2)
+        relay(group - 2, close)
     project_queries(5)
     loads[9].wait()
     wo_send.wait_recv()
     wo_pass.start()
-    pass_on(5)
-    for group in (3, 4, 5):
-        relay(group)
+    relay(4, close)
+    relay(5, close)
+    for group in range(len(groups)):
+        relay(group, crossing)
 
     for group in range(len(groups)):
         kv_copy(group, 0).wait_recv()
@@ -440,16 +445,18 @@
 
     for copy in sent:
         copy.wait_send()
-    for kind, there in ((0, None), (1, far_to), (2, close), (3, near), (4, crossing), (5, by_way)):
-
-        def finish():
-            for group in range(len(groups)):
-                kv_copy(group, kind).wait_send()
-
-        if there is None:
-            finish()
-        else:
-            pl.when(there)(finish)
+    for group in range(len(groups)):
+        detour = group < BY_WAY
+        kv_copy(group, 0).wait_send()
+        for kind, there in (
+            (1, far_to),
+            (2, close if detour else near),
+            (3, near),
+            (4, crossing),
+            (5, by_way),
+        ):
+            if kind < 4 or detour:
+                pl.when(there)(functools.partial(kv_copy(group, kind).wait_send))
 
 
 def per_device(

time: 67.3 us -> 59.9 us (0.89)
  Pallas kernels: 64.8 us -> 57.6 us
    pallas_call x1, Pallas kernels: 64.8 us -> 57.6 us  [per_device(): pl.pallas_call(functools.partial(kernel, lax.axis_size('frame')), out_sha...]
where the time goes in v4:
time: 59.9 us; the launch traced here: 59.7 us
  Pallas kernels  57.6 us (96%)
  other arithmetic  2.12 us (4%)
    pallas_call x1, Pallas kernels, per_device(): pl.pallas_call(functools.partial(kernel, lax.axis_size('frame')), out_sha...  57.6 us
    convert_element_type x1, other arithmetic, per_device(): return (own + from_right + from_left).astype(bf16)  2.12 us

profile of v4, /device:TPU:16, one launch (start us, length us, event | category | flops | bytes accessed | tf_op | source)
XLA Modules:
  0.0 59.7 jit_solution(18234358953857891722)
XLA Ops:
  0.0 57.6 %shard_map.100 = (bf16[64,3072]{1,0:T(8,128)(2,1)}, bf16[64,3072]{1,0:T(8,128)(2,1)}, bf16[64,3072]{1,0:T(8,128)(2,1)}) custom-call(bf16[64,3072]{1,0:T(8,128)(2,1)} %tokens_hbm.1, f32[1,3072]{1,0:T(1,128)} %bitcast.3, f32[1,128]{1,0:T(1,128)} %bitcast.4, f32[1,128]{1,0:T(1,128)} %bitcast.5, s32[4,6]{1,0:T(4,128)} %lists_hbm.1, s32[4]{0:T(128)} %counts_hbm.1, ...), custom_call_target="tpu_custom_call" | custom-call | tf_op jit(solution)/shard_map/pallas_call | solution.py:479
  57.6 2.1 %add_convert_fusion = bf16[64,3072]{1,0:T(8,128)(2,1)} fusion(bf16[64,3072]{1,0:T(8,128)(2,1)} %get-tuple-element.10, bf16[64,3072]{1,0:T(8,128)(2,1)} %get-tuple-element.9, bf16[64,3072]{1,0:T(8,128)(2,1)} %get-tuple-element.8), kind=kLoop, calls=%fused_computation | loop fusion | flops 1179648 | bytes 1572864 | tf_op jit(solution)/shard_map/convert_element_type | solution.py:529

commit v5 on v4

--- a/solution.py
+++ b/solution.py
@@ -14,7 +14,9 @@
 NB = 4
 EPS = 1e-06
 PIECES = 4
-BY_WAY = 2
+BY_WAY_UP = 0
+BY_WAY_DOWN = 2
+BY_WAY = max(BY_WAY_UP, BY_WAY_DOWN)
 MESH = pl.DeviceIdType.MESH
 
 SLOT = (0, 2, 1, 3)
@@ -89,7 +91,24 @@
         jnp.logical_and(f == mid - 1, core == 1), jnp.logical_and(f == mid, core == 0)
     )
     close = jnp.logical_and(near, jnp.logical_not(crossing))
+    spare = jnp.logical_or(f < 2, f >= frames - 2)
+    usual = jnp.logical_not(spare)
     by_way = jnp.logical_not(far_to)
+
+    def in_use(group, there, upper):
+        up = jnp.logical_and(upper == 1, group < BY_WAY_UP)
+        down = jnp.logical_and(upper == 0, group < BY_WAY_DOWN)
+        return jnp.logical_and(there, jnp.logical_or(up, down))
+
+    def cross_by_way(group):
+        return in_use(group, crossing, 1 - f // mid)
+
+    def passes(group):
+        return in_use(group, by_way, f // mid)
+
+    def near_directly(group):
+        return jnp.logical_and(near, jnp.logical_not(cross_by_way(group)))
+
     to_way = {"frame": f - toward * (mid - 1)}
     from_way = {"frame": f + toward * (mid - 2)}
     to_crossing = {"frame": f - toward * (mid - 2)}
@@ -164,9 +183,13 @@
 
     ag = (ag_s, ag_r)
     a_right, a_left, b_other, f_ward, c_right, c_left, d_other = [], [], [], [], [], [], []
+    c_full, e_other = [], []
+    depth = xn.shape[2]
+    cut = depth * 2 // 3
+    most, rest, every = pl.ds(0, cut), pl.ds(cut, depth - cut), pl.ds(0, depth)
     for p in range(PIECES):
         r = rows_of(p)
-        n = 7 * p
+        n = 8 * p
         a_right.append(send(xn.at[0, r], xn.at[3, r], ag, n, to_right))
         a_left.append(send(xn.at[0, r], xn.at[2, r], ag, n + 1, to_left))
         b_other.append(send(xn.at[0, r], xn.at[4, r], ag, n + 2, to_other))
@@ -174,9 +197,36 @@
             f_ward.append(send(xn.at[3, r], xn.at[1, r], ag, n + 3, to_right))
         else:
             f_ward.append(send(xn.at[2, r], xn.at[1, r], ag, n + 3, to_left))
-        c_right.append(send(xn.at[4, r], xn.at[7, r], ag, n + 4, to_right))
-        c_left.append(send(xn.at[4, r], xn.at[6, r], ag, n + 5, to_left))
-        d_other.append(send(xn.at[1, r], xn.at[5, r], ag, n + 6, to_other))
+        right_columns, left_columns = (most, every) if p % 2 else (every, most)
+        c_right.append(
+            send(xn.at[4, r, right_columns], xn.at[7, r, right_columns], ag, n + 4, to_right, False)
+        )
+        c_left.append(
+            send(xn.at[4, r, left_columns], xn.at[6, r, left_columns], ag, n + 5, to_left, False)
+        )
+        if p % 2:
+            c_full.append(send(xn.at[4, r], xn.at[7, r], ag, n + 4, to_right, False))
+            e_other.append(send(xn.at[3, r, rest], xn.at[7, r, rest], ag, n + 7, to_other, False))
+        else:
+            c_full.append(send(xn.at[4, r], xn.at[6, r], ag, n + 5, to_left, False))
+            e_other.append(send(xn.at[2, r, rest], xn.at[6, r, rest], ag, n + 7, to_other, False))
+        d_other.append(send(xn.at[1, r], xn.at[5, r], ag, n + 6, to_other, False))
+    g_right = send(xn.at[7, rows_of(2)], xn.at[5, rows_of(2)], ag, 22, to_right, False)
+    g_left = send(xn.at[6, rows_of(3)], xn.at[5, rows_of(3)], ag, 30, to_left, False)
+
+    def thrice(p, what):
+        (getattr(c_left[p], what) if p % 2 else getattr(c_right[p], what))()
+        cut_one = c_right[p] if p % 2 else c_left[p]
+
+        @pl.when(usual)
+        def _():
+            getattr(cut_one, what)()
+            if what != "start":
+                getattr(e_other[p], what)()
+
+        @pl.when(spare)
+        def _():
+            getattr(c_full[p], what)()
 
     def normed_heads(section, gain_ref):
         done = []
@@ -232,8 +282,8 @@
                 kv[at, low : low + each, i * HD : (i + 1) * HD] = pieces[i][r]
             kv[at, low : low + each, width:] = values[r]
         if group < BY_WAY:
-            pl.when(close)(lambda: kv_copy(group, 2).start())
-            pl.when(crossing)(lambda: kv_copy(group, 4).start())
+            pl.when(near_directly(group))(lambda: kv_copy(group, 2).start())
+            pl.when(cross_by_way(group))(lambda: kv_copy(group, 4).start())
         else:
             pl.when(near)(lambda: kv_copy(group, 2).start())
         pl.when(far_to)(lambda: kv_copy(group, 1).start())
@@ -250,7 +300,7 @@
                 ]
 
     def pass_on(group):
-        @pl.when(by_way)
+        @pl.when(passes(group))
         def _():
             kv_copy(group, 3).wait_recv()
             kv_copy(group, 5).start()
@@ -292,19 +342,23 @@
     for early, late in ((0, 1), (2, 3)):
         a_right[late].wait_recv()
         f_ward[late].start()
+        pl.when(usual)(e_other[late].start)
         a_left[early].wait_recv()
         f_ward[early].start()
-        for p in (early, late):
-            b_other[p].wait_recv()
-            c_right[p].start()
-            c_left[p].start()
+        pl.when(usual)(e_other[early].start)
+    for p in range(PIECES):
+        b_other[p].wait_recv()
+        thrice(p, "start")
     for p in (0, 2):
         a_right[p].wait_recv()
         a_left[p + 1].wait_recv()
     project_pairs(1)
     for p in range(PIECES):
         f_ward[p].wait_recv()
-        d_other[p].start()
+        if p < 2:
+            d_other[p].start()
+        else:
+            pl.when(usual)(d_other[p].start)
     pass_on(0)
     project_queries(1)
     project_pairs(2)
@@ -312,8 +366,12 @@
     relay(0, close)
     for first, last, group in ((0, 2, 3), (2, 3, 4), (3, 4, 5)):
         for p in range(first, last):
-            c_right[p].wait_recv()
-            c_left[p].wait_recv()
+            if group < 5:
+                thrice(p, "wait_recv")
+            if group == 4:
+                thrice(3, "wait_recv")
+                pl.when(spare)(g_right.start)
+                pl.when(spare)(g_left.start)
             d_other[p].wait_recv()
         project_pairs(group)
         if group - 2 < BY_WAY:
@@ -443,20 +501,18 @@
         c_r[(p + 2) % 4].wait_recv()
     mine.wait()
 
-    for copy in sent:
+    for copy in sent + d_other:
         copy.wait_send()
+    for p in range(PIECES):
+        thrice(p, "wait_send")
     for group in range(len(groups)):
-        detour = group < BY_WAY
         kv_copy(group, 0).wait_send()
-        for kind, there in (
-            (1, far_to),
-            (2, close if detour else near),
-            (3, near),
-            (4, crossing),
-            (5, by_way),
-        ):
-            if kind < 4 or detour:
-                pl.when(there)(functools.partial(kv_copy(group, kind).wait_send))
+        ends = ((1, far_to), (2, near), (3, near))
+        if group < BY_WAY:
+            ends = ((1, far_to), (2, near_directly(group)), (3, near))
+            ends += ((4, cross_by_way(group)), (5, passes(group)))
+        for kind, there in ends:
+            pl.when(there)(kv_copy(group, kind).wait_send)
 
 
 def per_device(
@@ -499,8 +555,8 @@
             pltpu.VMEM((4, rows, depth), bf16),
             pltpu.VMEM((rows, depth), bf16),
             dma((10,)),
-            dma((7 * PIECES,)),
-            dma((7 * PIECES,)),
+            dma((8 * PIECES,)),
+            dma((8 * PIECES,)),
             dma((24,)),
             dma((24,)),
             dma((2,)),

time: 59.9 us -> 60.7 us (1.013)
  the two profiles are of different devices: /device:TPU:16 before, /device:TPU:41 now
where the time goes in v5:
time: 60.7 us; the launch traced here: 60.5 us
  Pallas kernels  58.4 us (96%)
  other arithmetic  2.12 us (3%)
    pallas_call x1, Pallas kernels, per_device(): pl.pallas_call(functools.partial(kernel, lax.axis_size('frame')), out_sha...  58.4 us
    convert_element_type x1, other arithmetic, per_device(): return (own + from_right + from_left).astype(bf16)  2.12 us

profile of v5, /device:TPU:41, one launch (start us, length us, event | category | flops | bytes accessed | tf_op | source)
XLA Modules:
  0.0 60.5 jit_solution(14917825830322279051)
XLA Ops:
  0.0 58.4 %shard_map.100 = (bf16[64,3072]{1,0:T(8,128)(2,1)}, bf16[64,3072]{1,0:T(8,128)(2,1)}, bf16[64,3072]{1,0:T(8,128)(2,1)}) custom-call(bf16[64,3072]{1,0:T(8,128)(2,1)} %tokens_hbm.1, f32[1,3072]{1,0:T(1,128)} %bitcast.3, f32[1,128]{1,0:T(1,128)} %bitcast.4, f32[1,128]{1,0:T(1,128)} %bitcast.5, s32[4,6]{1,0:T(4,128)} %lists_hbm.1, s32[4]{0:T(128)} %counts_hbm.1, ...), custom_call_target="tpu_custom_call" | custom-call | tf_op jit(solution)/shard_map/pallas_call | solution.py:535
  58.4 2.1 %add_convert_fusion = bf16[64,3072]{1,0:T(8,128)(2,1)} fusion(bf16[64,3072]{1,0:T(8,128)(2,1)} %get-tuple-element.10, bf16[64,3072]{1,0:T(8,128)(2,1)} %get-tuple-element.9, bf16[64,3072]{1,0:T(8,128)(2,1)} %get-tuple-element.8), kind=kLoop, calls=%fused_computation | loop fusion | flops 1179648 | bytes 1572864 | tf_op jit(solution)/shard_map/convert_element_type | solution.py:585

commit v6 on v5

--- a/solution.py
+++ b/solution.py
@@ -93,6 +93,8 @@
     close = jnp.logical_and(near, jnp.logical_not(crossing))
     spare = jnp.logical_or(f < 2, f >= frames - 2)
     usual = jnp.logical_not(spare)
+    spare_all = f < 2
+    spare_half = jnp.logical_and(spare, f >= 2)
     by_way = jnp.logical_not(far_to)
 
     def in_use(group, there, upper):
@@ -213,6 +215,8 @@
         d_other.append(send(xn.at[1, r], xn.at[5, r], ag, n + 6, to_other, False))
     g_right = send(xn.at[7, rows_of(2)], xn.at[5, rows_of(2)], ag, 22, to_right, False)
     g_left = send(xn.at[6, rows_of(3)], xn.at[5, rows_of(3)], ag, 30, to_left, False)
+    g_first = send(xn.at[7, rows_of(0)], xn.at[5, rows_of(0)], ag, 6, to_right, False)
+    g_second = send(xn.at[6, rows_of(1)], xn.at[5, rows_of(1)], ag, 14, to_left, False)
 
     def thrice(p, what):
         (getattr(c_left[p], what) if p % 2 else getattr(c_right[p], what))()
@@ -355,10 +359,7 @@
     project_pairs(1)
     for p in range(PIECES):
         f_ward[p].wait_recv()
-        if p < 2:
-            d_other[p].start()
-        else:
-            pl.when(usual)(d_other[p].start)
+        pl.when(f >= 2 if p < 2 else usual)(d_other[p].start)
     pass_on(0)
     project_queries(1)
     project_pairs(2)
@@ -366,12 +367,29 @@
     relay(0, close)
     for first, last, group in ((0, 2, 3), (2, 3, 4), (3, 4, 5)):
         for p in range(first, last):
-            if group < 5:
+            if group == 3:
                 thrice(p, "wait_recv")
-            if group == 4:
+        if group == 3:
+
+            @pl.when(spare_all)
+            def _():
+                g_first.start()
+                g_second.start()
+                thrice(2, "wait_recv")
+                g_right.start()
                 thrice(3, "wait_recv")
-                pl.when(spare)(g_right.start)
-                pl.when(spare)(g_left.start)
+                g_left.start()
+
+        if group == 4:
+
+            @pl.when(f >= 2)
+            def _():
+                thrice(2, "wait_recv")
+                pl.when(spare_half)(g_right.start)
+                thrice(3, "wait_recv")
+                pl.when(spare_half)(g_left.start)
+
+        for p in range(first, last):
             d_other[p].wait_recv()
         project_pairs(group)
         if group - 2 < BY_WAY:

time: 60.7 us -> 59.6 us (0.982)
  the two profiles are of different devices: /device:TPU:41 before, /device:TPU:16 now
where the time goes in v6:
time: 59.6 us; the launch traced here: 59.1 us
  Pallas kernels  57 us (96%)
  other arithmetic  2.12 us (4%)
    pallas_call x1, Pallas kernels, per_device(): pl.pallas_call(functools.partial(kernel, lax.axis_size('frame')), out_sha...  57 us
    convert_element_type x1, other arithmetic, per_device(): return (own + from_right + from_left).astype(bf16)  2.12 us

profile of v6, /device:TPU:16, one launch (start us, length us, event | category | flops | bytes accessed | tf_op | source)
XLA Modules:
  0.0 59.1 jit_solution(7495038697172916594)
XLA Ops:
  0.0 57.0 %shard_map.100 = (bf16[64,3072]{1,0:T(8,128)(2,1)}, bf16[64,3072]{1,0:T(8,128)(2,1)}, bf16[64,3072]{1,0:T(8,128)(2,1)}) custom-call(bf16[64,3072]{1,0:T(8,128)(2,1)} %tokens_hbm.1, f32[1,3072]{1,0:T(1,128)} %bitcast.3, f32[1,128]{1,0:T(1,128)} %bitcast.4, f32[1,128]{1,0:T(1,128)} %bitcast.5, s32[4,6]{1,0:T(4,128)} %lists_hbm.1, s32[4]{0:T(128)} %counts_hbm.1, ...), custom_call_target="tpu_custom_call" | custom-call | tf_op jit(solution)/shard_map/pallas_call | solution.py:553
  57.0 2.1 %add_convert_fusion = bf16[64,3072]{1,0:T(8,128)(2,1)} fusion(bf16[64,3072]{1,0:T(8,128)(2,1)} %get-tuple-element.10, bf16[64,3072]{1,0:T(8,128)(2,1)} %get-tuple-element.9, bf16[64,3072]{1,0:T(8,128)(2,1)} %get-tuple-element.8), kind=kLoop, calls=%fused_computation | loop fusion | flops 1179648 | bytes 1572864 | tf_op jit(solution)/shard_map/convert_element_type | solution.py:603

commit v7 on v6

--- a/solution.py
+++ b/solution.py
@@ -95,6 +95,8 @@
     usual = jnp.logical_not(spare)
     spare_all = f < 2
     spare_half = jnp.logical_and(spare, f >= 2)
+    whole = jnp.logical_or(spare_half, f // 2 == mid // 2)
+    cut_some = jnp.logical_not(whole)
     by_way = jnp.logical_not(far_to)
 
     def in_use(group, there, upper):
@@ -222,13 +224,13 @@
         (getattr(c_left[p], what) if p % 2 else getattr(c_right[p], what))()
         cut_one = c_right[p] if p % 2 else c_left[p]
 
-        @pl.when(usual)
+        @pl.when(cut_some)
         def _():
             getattr(cut_one, what)()
             if what != "start":
                 getattr(e_other[p], what)()
 
-        @pl.when(spare)
+        @pl.when(whole)
         def _():
             getattr(c_full[p], what)()
 
@@ -346,10 +348,10 @@
     for early, late in ((0, 1), (2, 3)):
         a_right[late].wait_recv()
         f_ward[late].start()
-        pl.when(usual)(e_other[late].start)
+        pl.when(cut_some)(e_other[late].start)
         a_left[early].wait_recv()
         f_ward[early].start()
-        pl.when(usual)(e_other[early].start)
+        pl.when(cut_some)(e_other[early].start)
     for p in range(PIECES):
         b_other[p].wait_recv()
         thrice(p, "start")

time: 59.6 us -> 59.2 us (level)
  no operation moved by 1% of the time
where the time goes in v7:
time: 59.2 us; the launch traced here: 59.1 us
  Pallas kernels  57 us (96%)
  other arithmetic  2.12 us (4%)
    pallas_call x1, Pallas kernels, per_device(): pl.pallas_call(functools.partial(kernel, lax.axis_size('frame')), out_sha...  57 us
    convert_element_type x1, other arithmetic, per_device(): return (own + from_right + from_left).astype(bf16)  2.12 us

profile of v7, /device:TPU:16, one launch (start us, length us, event | category | flops | bytes accessed | tf_op | source)
XLA Modules:
  0.0 59.1 jit_solution(9705815888996776833)
XLA Ops:
  0.0 57.0 %shard_map.100 = (bf16[64,3072]{1,0:T(8,128)(2,1)}, bf16[64,3072]{1,0:T(8,128)(2,1)}, bf16[64,3072]{1,0:T(8,128)(2,1)}) custom-call(bf16[64,3072]{1,0:T(8,128)(2,1)} %tokens_hbm.1, f32[1,3072]{1,0:T(1,128)} %bitcast.3, f32[1,128]{1,0:T(1,128)} %bitcast.4, f32[1,128]{1,0:T(1,128)} %bitcast.5, s32[4,6]{1,0:T(4,128)} %lists_hbm.1, s32[4]{0:T(128)} %counts_hbm.1, ...), custom_call_target="tpu_custom_call" | custom-call | tf_op jit(solution)/shard_map/pallas_call | solution.py:555
  57.0 2.1 %add_convert_fusion = bf16[64,3072]{1,0:T(8,128)(2,1)} fusion(bf16[64,3072]{1,0:T(8,128)(2,1)} %get-tuple-element.10, bf16[64,3072]{1,0:T(8,128)(2,1)} %get-tuple-element.9, bf16[64,3072]{1,0:T(8,128)(2,1)} %get-tuple-element.8), kind=kLoop, calls=%fused_computation | loop fusion | flops 1179648 | bytes 1572864 | tf_op jit(solution)/shard_map/convert_element_type | solution.py:605

commit v8 on v7

--- a/solution.py
+++ b/solution.py
@@ -466,6 +466,9 @@
 
     def out_project(k):
         partial = jnp.dot(ctx[k, 0], wo[0:width], preferred_element_type=jnp.float32)
+        ctx_sends[k].wait_recv()
+        if k == 2:
+            wo_pass.wait_recv()
         partial = partial + jnp.dot(ctx[k, 2], wo[width:], preferred_element_type=jnp.float32)
         part[k] = partial.astype(jnp.bfloat16)
 
@@ -483,19 +486,15 @@
     for k in (2, 3, 1):
         attend(k)
         ctx_sends[k].start()
-    wo_pass.wait_recv()
-    ctx_sends[2].wait_recv()
     out_project(2)
     for p in range(2):
         h_left[p].start()
         h_right[p].start()
     attend(0)
     ctx_sends[0].start()
-    ctx_sends[3].wait_recv()
     out_project(3)
     c_l[2].start()
     c_l[3].start()
-    ctx_sends[1].wait_recv()
     out_project(1)
     c_r[0].start()
     c_r[1].start()
@@ -512,7 +511,6 @@
         h_right[p].wait_recv()
         add_in(1, p + 2)
         c_r[p + 2].start()
-    ctx_sends[0].wait_recv()
     out_project(0)
     mine = pltpu.make_async_copy(part.at[0], own_hbm, in_sem.at[0])
     mine.start()

time: 59.2 us -> 59.2 us (level)
  no operation moved by 1% of the time
where the time goes in v8:
time: 59.2 us; the launch traced here: 59.1 us
  Pallas kernels  57 us (96%)
  other arithmetic  2.12 us (4%)
    pallas_call x1, Pallas kernels, per_device(): pl.pallas_call(functools.partial(kernel, lax.axis_size('frame')), out_sha...  57 us
    convert_element_type x1, other arithmetic, per_device(): return (own + from_right + from_left).astype(bf16)  2.12 us

profile of v8, /device:TPU:16, one launch (start us, length us, event | category | flops | bytes accessed | tf_op | source)
XLA Modules:
  0.0 59.1 jit_solution(9963918026288061234)
XLA Ops:
  0.0 57.0 %shard_map.100 = (bf16[64,3072]{1,0:T(8,128)(2,1)}, bf16[64,3072]{1,0:T(8,128)(2,1)}, bf16[64,3072]{1,0:T(8,128)(2,1)}) custom-call(bf16[64,3072]{1,0:T(8,128)(2,1)} %tokens_hbm.1, f32[1,3072]{1,0:T(1,128)} %bitcast.3, f32[1,128]{1,0:T(1,128)} %bitcast.4, f32[1,128]{1,0:T(1,128)} %bitcast.5, s32[4,6]{1,0:T(4,128)} %lists_hbm.1, s32[4]{0:T(128)} %counts_hbm.1, ...), custom_call_target="tpu_custom_call" | custom-call | tf_op jit(solution)/shard_map/pallas_call | solution.py:553
  57.0 2.1 %add_convert_fusion = bf16[64,3072]{1,0:T(8,128)(2,1)} fusion(bf16[64,3072]{1,0:T(8,128)(2,1)} %get-tuple-element.10, bf16[64,3072]{1,0:T(8,128)(2,1)} %get-tuple-element.9, bf16[64,3072]{1,0:T(8,128)(2,1)} %get-tuple-element.8), kind=kLoop, calls=%fused_computation | loop fusion | flops 1179648 | bytes 1572864 | tf_op jit(solution)/shard_map/convert_element_type | solution.py:603
